TPU v7x, 128 devices: a whole 4x4x4 slice. The times are simulated.
128 devices in a mesh: replica: 16 (over x, y), tensor: 8 (over z, core).
Axes of the slice: x: 4, y: 4, z: 4, core: 2. Of those that a mesh axis runs over, the one named last changes fastest.
Arguments:
- hidden: bfloat16 [2048, 8192], P('replica', 'tensor'), may hold values from -6 to 6
- query_weight: bfloat16 [8192, 4096], P(None, 'tensor'), may hold values from -0.0625 to 0.0625
- keyvalue_weight: bfloat16 [2, 8192, 1024], P(None, None, 'tensor'), may hold values from -0.0625 to 0.0625
- output_weight: bfloat16 [4096, 8192], P('tensor'), may hold values from -0.09375 to 0.09375
- adapter_down_maps: bfloat16 [128, 8192, 48], P('replica', 'tensor'), may hold values from -0.0625 to 0.0625
- adapter_up_query: bfloat16 [128, 16, 4096], P('replica', None, 'tensor'), may hold values from -0.375 to 0.375
- adapter_up_keyvalue: bfloat16 [128, 2, 16, 1024], P('replica', None, None, 'tensor'), may hold values from -0.375 to 0.375
- adapter_down_output: bfloat16 [128, 4096, 16], P('replica', 'tensor'), may hold values from -0.09375 to 0.09375
- adapter_up_output: bfloat16 [128, 16, 8192], P('replica', None, 'tensor'), may hold values from -0.375 to 0.375
- cached_keys: bfloat16 [2048, 8, 128, 128], P('replica', 'tensor'), may hold values from -420 to 420
- cached_values: bfloat16 [2048, 8, 128, 128], P('replica', 'tensor'), may hold values from -18 to 18
- context_lengths: int32 [2048], P('replica'), may hold values from 2 to 128, as said below
- request_list_slots: int32 [2048], P('replica'), may hold values from 0 to 31
- group_adapter_lists: int32 [16, 32], replicated, may hold values from 0 to 127, as said below
Outputs:
- mixed_out: bfloat16 [2048, 8192], P('replica', 'tensor')
Inputs may be any that keep to these rules, and one draw needn't show every extreme that they name: `context_lengths`: in every group of 128 consecutive requests one has exactly 128. `group_adapter_lists`: each row names 32 different adapters; at most 4 of a row lie in one block of 8 consecutive adapter numbers, and in every row some block holds exactly 4.
All inputs are finite; a program needn't handle non-finite values.
Results may differ from a plain program's by a relative error of at most 0.012.
The roundings to bfloat16 on the way count: a program that leaves them out, or rounds other values in their place, can miss the bound.
Values may be sent and summed in bfloat16 or wider, within the bound.
A program may use at most 128 MiB of HBM per device.

v0:
```python
import jax
import jax.numpy as jnp
from jax import lax
from jax.sharding import PartitionSpec as P

ADAPTER_SCALE = 2.0
ROPE_BASE = 500000.0


def rotate(values, positions):
    half_size = values.shape[-1] // 2
    frequency = ROPE_BASE ** (-(jnp.arange(half_size, dtype=jnp.float32) * 2.0) / values.shape[-1])
    angles = positions.astype(jnp.float32)[:, None, None] * frequency[None, None, :]
    cosine_terms = jnp.cos(angles)
    sine_terms = jnp.sin(angles)
    front = values[..., :half_size]
    back = values[..., half_size:]
    return jnp.concatenate(
        [front * cosine_terms - back * sine_terms, back * cosine_terms + front * sine_terms],
        axis=-1,
    )


def attend(queries, new_key, new_value, cached_keys, cached_values, context_lengths):
    score_scale = 1.0 / jnp.sqrt(jnp.float32(queries.shape[-1]))
    scores = (
        jnp.einsum("rkgh,rkch->rkgc", queries, cached_keys, preferred_element_type=jnp.float32)
        * score_scale
    )
    self_score = (
        jnp.einsum("rkgh,rkh->rkg", queries, new_key, preferred_element_type=jnp.float32)
        * score_scale
    )
    valid = (jnp.arange(cached_keys.shape[2], dtype=jnp.int32)[None, :] < context_lengths[:, None])[
        :, None, None, :
    ]
    highest = jnp.maximum(jnp.max(jnp.where(valid, scores, -1e30), axis=-1), self_score)
    weights = jnp.where(valid, jnp.exp(scores - highest[..., None]), 0.0)
    self_weight = jnp.exp(self_score - highest)
    total = jnp.sum(weights, axis=-1) + self_weight
    rounded = (weights / total[..., None]).astype(jnp.bfloat16)
    self_rounded = (self_weight / total).astype(jnp.bfloat16)
    mixed = jnp.einsum(
        "rkgc,rkch->rkgh", rounded, cached_values, preferred_element_type=jnp.float32
    )
    mixed = (
        mixed
        + self_rounded.astype(jnp.float32)[..., None] * new_value.astype(jnp.float32)[:, :, None, :]
    )
    return mixed.astype(jnp.bfloat16).reshape(queries.shape[0], -1)


def shards(
    hidden,
    query_weight,
    keyvalue_weight,
    output_weight,
    adapter_down_maps,
    adapter_up_query,
    adapter_up_keyvalue,
    adapter_down_output,
    adapter_up_output,
    cached_keys,
    cached_values,
    context_lengths,
    request_list_slots,
    group_adapter_lists,
):
    request_rows = hidden.shape[0]
    head_size = cached_keys.shape[3]
    kv_local = cached_keys.shape[1]
    rank_width = adapter_up_query.shape[1]
    segment = lax.all_gather(hidden, "tensor", axis=1, tiled=True)
    frozen_query = jnp.dot(segment, query_weight, preferred_element_type=jnp.float32)
    frozen_keyvalue = jnp.einsum(
        "rd,cdk->crk", segment, keyvalue_weight, preferred_element_type=jnp.float32
    )
    group_index = lax.axis_index("replica")
    wanted = lax.dynamic_index_in_dim(group_adapter_lists, group_index, 0, keepdims=False)
    zero_half = jnp.zeros((), jnp.bfloat16)
    gathered = (
        lax.all_gather(adapter_down_maps, "replica", axis=0, tiled=True),
        lax.all_gather(adapter_up_query, "replica", axis=0, tiled=True),
        lax.all_gather(adapter_up_keyvalue, "replica", axis=0, tiled=True),
        lax.all_gather(adapter_down_output, "replica", axis=0, tiled=True),
        lax.all_gather(adapter_up_output, "replica", axis=0, tiled=True),
    )
    chosen = jax.tree.map(lambda member: jnp.take(member, wanted, axis=0), gathered)
    sel_down, sel_up_q, sel_up_kv, sel_down_o, sel_up_o = chosen
    count = sel_down.shape[0]
    chosen_mask = request_list_slots[:, None] == jnp.arange(count)[None, :]
    every_rank = jnp.einsum("rd,ldk->rlk", hidden, sel_down, preferred_element_type=jnp.float32)
    part_rank = jnp.sum(jnp.where(chosen_mask[:, :, None], every_rank, 0.0), axis=1)
    reduced_rows = lax.psum(part_rank, "tensor").astype(jnp.bfloat16)
    expanded = jnp.where(chosen_mask[:, :, None], reduced_rows[:, None, :], zero_half)
    raised_query = jnp.einsum(
        "rlk,lkq->rq", expanded[:, :, :rank_width], sel_up_q, preferred_element_type=jnp.float32
    )
    raised_keyvalue = jnp.einsum(
        "rlck,lckv->crv",
        expanded[:, :, rank_width:].reshape(request_rows, count, 2, rank_width),
        sel_up_kv,
        preferred_element_type=jnp.float32,
    )
    unrotated_query = frozen_query + ADAPTER_SCALE * raised_query
    unrotated_keyvalue = frozen_keyvalue + ADAPTER_SCALE * raised_keyvalue
    queries = rotate(unrotated_query.reshape(request_rows, -1, head_size), context_lengths).astype(
        jnp.bfloat16
    )
    queries = queries.reshape(request_rows, kv_local, -1, head_size)
    new_key = rotate(
        unrotated_keyvalue[0].reshape(request_rows, kv_local, head_size), context_lengths
    ).astype(jnp.bfloat16)
    new_value = (
        unrotated_keyvalue[1].reshape(request_rows, kv_local, head_size).astype(jnp.bfloat16)
    )
    attention_output = attend(
        queries, new_key, new_value, cached_keys, cached_values, context_lengths
    )
    partial_value = jnp.dot(attention_output, output_weight, preferred_element_type=jnp.float32)
    combined_output = lax.psum_scatter(partial_value, "tensor", scatter_dimension=1, tiled=True)
    every_out = jnp.einsum(
        "rq,lqk->rlk", attention_output, sel_down_o, preferred_element_type=jnp.float32
    )
    part_out = jnp.sum(jnp.where(chosen_mask[:, :, None], every_out, 0.0), axis=1)
    reduced_output = lax.psum(part_out, "tensor").astype(jnp.bfloat16)
    expanded_out = jnp.where(chosen_mask[:, :, None], reduced_output[:, None, :], zero_half)
    raised_output = jnp.einsum(
        "rlk,lkd->rd", expanded_out, sel_up_o, preferred_element_type=jnp.float32
    )
    return (combined_output + ADAPTER_SCALE * raised_output).astype(jnp.bfloat16)


def solution(mesh):
    in_specs = (
        P("replica", "tensor"),
        P(None, "tensor"),
        P(None, None, "tensor"),
        P("tensor", None),
        P("replica", "tensor", None),
        P("replica", None, "tensor"),
        P("replica", None, None, "tensor"),
        P("replica", "tensor", None),
        P("replica", None, "tensor"),
        P("replica", "tensor", None, None),
        P("replica", "tensor", None, None),
        P("replica"),
        P("replica"),
        P(),
    )
    out_specs = P("replica", "tensor")
    return jax.shard_map(shards, mesh=mesh, in_specs=in_specs, out_specs=out_specs, check_vma=False)
```

profile of v0, /device:TPU:0, one launch (start us, length us, event | category | flops | bytes accessed | tf_op | source)
XLA Modules:
  0.0 368.7 jit_solution(13590433030765379388)
XLA Ops:
  6.5 0.7 all-gather.13.cloned.1.call-update
  7.3 0.7 all-gather.7.cloned.1.call-update
  8.1 0.7 all-gather.11.cloned.1.call-update
  8.8 0.5 all-gather.9.cloned.1.call-update
  9.4 0.5 all-gather.15.cloned.1.call-update
  10.5 0.7 convert_element_type.58
  11.2 0.7 fusion.76
  11.9 1.2 compare_and_fusion
  13.1 1.3 iota_compare_fusion.1
  14.4 0.7 iota_compare_fusion
  15.4 39.1 %all-gather.13.cloned.1.call-done = bf16[128,2,16,128]{3,2,1,0:T(8,128)(2,1)} async-done(((bf16[8,2,16,128]{3,2,1,0:T(8,128)(2,1)}), bf16[128,2,16,128]{3,2,1,0:T(8,128)(2,1)}) %all-gather.13.cloned.1.call-update) | async-done | bytes 1048592 | tf_op jit(solution)/shard_map/all_gather | solution.py:84
  54.6 2.5 gather_fusion.2
  57.1 23.9 %all-gather.7.cloned.1.call-done = bf16[128,8192]{1,0:T(8,128)(2,1)} async-done(((bf16[128,1024]{1,0:T(8,128)(2,1)}), bf16[128,8192]{1,0:T(8,128)(2,1)}) %all-gather.7.cloned.1.call-update) | async-done | bytes 2097168 | tf_op jit(solution)/shard_map/all_gather | solution.py:73
  81.0 5.3 %fusion.83 = f32[128,512]{1,0:T(8,128)S(1)} fusion(bf16[128,8192]{1,0:T(8,128)(2,1)} %all-gather.7.cloned.1.call-done, bf16[8192,512]{1,0:T(8,128)(2,1)} %param.15), kind=kOutput, calls=%fused_computation.104 | convolution fusion | flops 1073741824 | bytes 10747904 | tf_op jit(solution)/shard_map/dot_general | solution.py:74
  86.3 42.0 %all-gather.11.cloned.1.call-done = bf16[128,16,512]{2,1,0:T(8,128)(2,1)} async-done(((bf16[8,16,512]{2,1,0:T(8,128)(2,1)}), bf16[128,16,512]{2,1,0:T(8,128)(2,1)}) %all-gather.11.cloned.1.call-update) | async-done | bytes 2097168 | tf_op jit(solution)/shard_map/all_gather | solution.py:83
  128.3 3.0 gather_fusion.1
  131.3 88.4 %all-gather.9.cloned.1.call-done = bf16[128,1024,48]{1,2,0:T(8,128)(2,1)} async-done(((bf16[8,1024,48]{1,2,0:T(8,128)(2,1)}), bf16[128,1024,48]{1,2,0:T(8,128)(2,1)}) %all-gather.9.cloned.1.call-update) | async-done | bytes 12582928 | tf_op jit(solution)/shard_map/all_gather | solution.py:82
  219.6 5.4 %gather_fusion = bf16[32,1024,48]{1,2,0:T(8,128)(2,1)S(1)} fusion(bf16[128,1024,48]{1,2,0:T(8,128)(2,1)} %all-gather.9.cloned.1.call-done, s32[1024]{0:T(1024)} %copy-done.2), kind=kCustom, calls=%fused_computation | custom fusion | bytes 6291584 | tf_op jit(solution)/shard_map/jit(_take)/gather | solution.py:88
  225.1 2.6 fusion.19
  227.7 26.5 %psum.14 = bf16[128,48]{0,1:T(8,128)(2,1)S(1)} all-reduce(f32[128,48]{0,1:T(8,128)} %fusion.19), channel_id=1, replica_groups=mesh['replica'=16,'tensor'=8] {'tensor'}, use_global_device_ids=true, to_apply=%region_1.2 | all-reduce | flops 6144 | bytes 36864 | tf_op jit(solution)/shard_map/psum | solution.py:94
  254.2 0.7 broadcast_select_fusion.2
  254.9 1.3 fusion.40
  256.3 4.3 %fusion.37 = f32[2,128,128]{1,2,0:T(8,128)S(1)} fusion(f32[2,128,128]{1,2,0:T(8,128)S(1)} %fusion.40, bf16[2,8192,128]{2,1,0:T(8,128)(2,1)} %param.16, bf16[128,8192]{1,0:T(8,128)(2,1)} %all-gather.7.cloned.1.call-done), kind=kOutput, calls=%fused_computation.31 | convolution fusion | flops 536903680 | bytes 6553600 | tf_op jit(solution)/shard_map/rd,cdk->crk/dot_general | solution.py:75
  262.1 4.7 %select_reduce_fusion = (f32[128,4]{1,0:T(8,128)S(1)}, f32[128,4,128]{2,1,0:T(4,128)S(1)}) fusion(pred[128,128]{1,0:T(8,128)(4,1)S(1)} %iota_compare_fusion, bf16[128,1,128,128]{3,2,1,0:T(8,128)(2,1)} %param.23, bf16[128,4,64]{2,1,0:T(4,128)(2,1)S(1)} %get-tuple-element.6, bf16[128,4,64]{2,1,0:T(4,128)(2,1)S(1)} %get-tuple-element.5), kind=kOutput, calls=%fused_computation.45 | convolution fusion | flops 17235456 | bytes 4605952 | tf_op jit(solution)/shard_map/rkgh,rkch->rkgc/dot_general | solution.py:27
  267.8 3.5 fusion.30
  271.3 6.6 %fusion.50 = f32[128,8192]{1,0:T(8,128)} fusion(bf16[512,8192]{1,0:T(8,128)(2,1)} %param.17, bf16[16,8,4,128]{3,2,1,0:T(4,128)(2,1)S(1)} %bitcast.82), kind=kOutput, calls=%fused_computation.52 | convolution fusion | flops 1073741824 | bytes 12713984 | tf_op jit(solution)/shard_map/dot_general | solution.py:120
  277.9 2.4 gather_fusion.3
  280.4 38.6 %all-gather.17.cloned.1.call-done = bf16[128,16,1024]{2,1,0:T(8,128)(2,1)} async-done(((bf16[8,16,1024]{2,1,0:T(8,128)(2,1)}), bf16[128,16,1024]{2,1,0:T(8,128)(2,1)}) %all-gather.17.cloned.1.call-update) | async-done | bytes 4194320 | tf_op jit(solution)/shard_map/all_gather | solution.py:86
  319.0 2.9 gather_fusion.4
  322.6 15.2 %psum.15 = bf16[128,16]{0,1:T(8,128)(2,1)S(1)} all-reduce(f32[128,16]{0,1:T(8,128)S(1)} %fusion.33), channel_id=1, replica_groups=mesh['replica'=16,'tensor'=8] {'tensor'}, use_global_device_ids=true, to_apply=%region_6.7 | all-reduce | flops 2048 | bytes 12288 | tf_op jit(solution)/shard_map/psum | solution.py:126
  337.9 21.5 %reduce-scatter.2.cloned.1.call-done = f32[128,1024]{1,0:T(8,128)} async-done(((f32[128,8192]{1,0:T(8,128)}), f32[128,1024]{1,0:T(8,128)}) %reduce-scatter.2.cloned.1.call-update) | async-done | bytes 524304 | tf_op jit(solution)/shard_map/reduce_scatter | solution.py:121
  359.4 2.5 fusion.18
  (53 shorter events, 4.4 us)
Async XLA Ops:
  6.5 48.0 %all-gather.13.cloned.1.call-start = ((), (), s32[]{:S(2)}) async-start(), calls=%async_computation.4 | async-start | bytes 1114112 | tf_op jit(solution)/shard_map/all_gather | solution.py:84
  7.3 73.7 %all-gather.7.cloned.1.call-start = ((), (), s32[]{:S(2)}) async-start(), calls=%async_computation.1 | async-start | bytes 2359296 | tf_op jit(solution)/shard_map/all_gather | solution.py:73
  8.0 120.3 %all-gather.11.cloned.1.call-start = ((), (), s32[]{:S(2)}) async-start(), calls=%async_computation.3 | async-start | bytes 2228224 | tf_op jit(solution)/shard_map/all_gather | solution.py:83
  8.7 210.9 %all-gather.9.cloned.1.call-start = ((), (), s32[]{:S(2)}) async-start(), calls=%async_computation.2 | async-start | bytes 13369344 | tf_op jit(solution)/shard_map/all_gather | solution.py:82
  9.3 268.6 %all-gather.15.cloned.1.call-start = ((), (), s32[]{:S(2)}) async-start(), calls=%async_computation.6 | async-start | bytes 2228224 | tf_op jit(solution)/shard_map/all_gather | solution.py:85
  9.9 309.1 %all-gather.17.cloned.1.call-start = ((), (), s32[]{:S(2)}) async-start(), calls=%async_computation.7 | async-start | bytes 4456448 | tf_op jit(solution)/shard_map/all_gather | solution.py:86
  10.5 348.9 %reduce-scatter.2.cloned.1.call-start = ((), (), s32[]{:S(2)}) async-start(), calls=%async_computation.5 | async-start | bytes 4718592 | tf_op jit(solution)/shard_map/reduce_scatter | solution.py:121
  11.2 75.0 %copy-start.4 = (f32[128]{0:T(128)}, f32[128]{0:T(128)S(1)}, u32[]{:S(2)}) copy-start(f32[128]{0:T(128)S(1)} %convert_element_type.58) | copy-start | bytes 1540
  13.1 73.2 %copy-start.6 = (f32[64]{0:T(128)}, f32[64]{0:T(128)S(1)}, u32[]{:S(2)}) copy-start(f32[64]{0:T(128)S(1)} %multiply_power_fusion) | copy-start | bytes 772
  13.1 115.2 %copy-start.2 = (s32[1024]{0:T(1024)}, s32[1024]{0:T(1024)S(1)}, u32[]{:S(2)}) copy-start(s32[1024]{0:T(1024)S(1)} %pad_clamp_fusion) | copy-start | bytes 12292
  256.2 4.4 %copy-start.5 = (f32[128]{0:T(128)S(1)}, f32[128]{0:T(128)}, u32[]{:S(2)}) copy-start(f32[128]{0:T(128)} %copy-done.4) | copy-start | bytes 1540
  256.2 4.4 %copy-start.7 = (f32[64]{0:T(128)S(1)}, f32[64]{0:T(128)}, u32[]{:S(2)}) copy-start(f32[64]{0:T(128)} %copy-done.6) | copy-start | bytes 772
  256.2 4.7 %copy-start = (bf16[32,16,512]{2,1,0:T(8,128)(2,1)S(1)}, bf16[32,16,512]{2,1,0:T(8,128)(2,1)}, u32[]{:S(2)}) copy-start(bf16[32,16,512]{2,1,0:T(8,128)(2,1)} %gather_fusion.1) | copy-start | bytes 1572868
  256.3 4.7 %copy-start.3 = (pred[32]{0:T(512)(128)(4,1)S(1)}, pred[32]{0:T(512)(128)(4,1)}, u32[]{:S(2)}) copy-start(pred[32]{0:T(512)(128)(4,1)} %compare_and_fusion) | copy-start | bytes 100
  280.3 41.9 %copy-start.1 = (pred[128,32]{0,1:T(8,128)(4,1)S(1)}, pred[128,32]{0,1:T(8,128)(4,1)}, u32[]{:S(2)}) copy-start(pred[128,32]{0,1:T(8,128)(4,1)} %iota_compare_fusion.1) | copy-start | bytes 12292
Sparse Core Ops, SparseCore 0:
  9.5 45.0 all-gather.12
  56.3 24.6 all-gather.6
  83.1 45.1 all-gather.10
  130.3 89.2 all-gather.8
  221.6 44.4 all-gather.14
  268.2 50.7 all-gather.16
  321.4 37.9 reduce-scatter.1
where the time goes:
time: 369 us
  waiting for transfers between devices  257 us (70%)
  blocking collectives  41.7 us (11%)
  matrix products  31.5 us (9%)
  local copies, waits for them, and re-layouts  17.1 us (5%)
  between operations  13.8 us (4%)
  other arithmetic  7.1 us (2%)
    all_gather x1, waiting for transfers between devices, shards(): lax.all_gather(adapter_down_maps, 'replica', axis=0, tiled=True)  88.4 us
    all_gather x1, waiting for transfers between devices, shards(): lax.all_gather(adapter_up_query, 'replica', axis=0, tiled=True)  42 us
    all_gather x1, waiting for transfers between devices, shards(): lax.all_gather(adapter_up_keyvalue, 'replica', axis=0, tiled=True)  39.1 us
    all_gather x1, waiting for transfers between devices, shards(): lax.all_gather(adapter_up_output, 'replica', axis=0, tiled=True)  38.6 us
    psum x1, blocking collectives, shards(): reduced_rows = lax.psum(part_rank, 'tensor').astype(jnp.bfloat16)  26.5 us
    all_gather x1, waiting for transfers between devices, shards(): segment = lax.all_gather(hidden, 'tensor', axis=1, tiled=True)  23.9 us
    reduce_scatter x1, waiting for transfers between devices, shards(): lax.psum_scatter(partial_value, 'tensor', scatter_dimension=1, tiled=True)  21.5 us
    gather x5, local copies, waits for them, and re-layouts, shards(): jnp.take(member, wanted, axis=0)  16.2 us
  transfers between devices with their start and end apart: 7, of which 6 were waited for; matrix products, arithmetic and copies ran while one was open for 14% of the time, Pallas kernels for 0%

commit v1 on v0

v1 whole, which is shorter than its diff:
```python
import functools

import jax
import jax.numpy as jnp
from jax import lax
from jax.experimental import pallas as pl
from jax.experimental.pallas import tpu as pltpu
from jax.sharding import PartitionSpec as P

ADAPTER_SCALE = 2.0
ROPE_BASE = 500000.0
MESH = pl.DeviceIdType.MESH
BF16 = jnp.bfloat16
F32 = jnp.float32
NT = (((1,), (1,)), ((), ()))
NEGATIVE = -1e30
SENDS = 104
LOCALS = 56


def mm(a, b):
    return jnp.dot(a, b, preferred_element_type=F32)


def kernel(
    hidden, ids_rows, ids_col, cosines, sines, lengths,
    query_w, kv_w, out_w, down, up_q, up_kv, down_o, up_o, keys, values,
    out,
    z_all, h_a, h_b, d_a, d_b, u_all, p_all, o_all, w_all, w_out, k_all, v_all,
    acc, low_send_a, low_recv_a, low_send_b, low_recv_b, low_parts, out_parts,
    q_rows, key_rows, value_rows, length_rows, mixed_rows,
    sib_send, sib_recv, far_send, far_plus, far_minus, near_send, near_recv, own_sum,
    send_sem, recv_sem, local_sem,
):
    replica = lax.axis_index("replica")
    t = lax.axis_index("tensor")
    x, y = replica // 4, replica % 4
    z, c = t // 2, t % 2
    other = 1 - c

    def wrap(v):
        return lax.rem(v + 4, 4)

    def at_x(d):
        return (wrap(x + d) * 4 + y, t)

    def at_y(d):
        return (x * 4 + wrap(y + d), t)

    def at_z(d):
        return (replica, wrap(z + d) * 2 + c)

    sibling = (replica, z * 2 + other)

    counts = {"send": 0, "local": 0}
    sent = []

    def send(src, dst, device):
        i = counts["send"]
        counts["send"] = i + 1
        copy = pltpu.make_async_remote_copy(
            src_ref=src, dst_ref=dst, send_sem=send_sem.at[i], recv_sem=recv_sem.at[i],
            device_id=device, device_id_type=MESH,
        )
        copy.start()
        sent.append(copy)
        return copy

    def local(src, dst):
        i = counts["local"]
        counts["local"] = i + 1
        copy = pltpu.make_async_copy(src, dst, local_sem.at[i])
        copy.start()
        return copy

    barrier = pltpu.get_barrier_semaphore()
    partners = [at_x(d) for d in (1, 2, 3)] + [at_y(d) for d in (1, 2, 3)]
    partners += [(replica, lax.rem(t + d, 8)) for d in range(1, 8)]
    for partner in partners:
        pl.semaphore_signal(barrier, inc=1, device_id=partner, device_id_type=MESH)

    own_h = [
        local(hidden, z_all.at[t]),
        local(hidden.at[:, 0:512], h_a.at[x, 0:128]),
        local(ids_rows, h_a.at[x, 128:144]),
        local(hidden.at[:, 512:1024], h_b.at[y, 0:128]),
        local(ids_rows, h_b.at[y, 128:144]),
    ]
    own_d = [
        local(down.at[:, :, 0:512], d_a.at[y]),
        local(down.at[:, :, 512:1024], d_b.at[x]),
    ]
    own_u = [
        local(up_q, u_all.at[x, y, :, :, 0:512]),
        local(up_kv.at[:, 0], u_all.at[x, y, :, :, 512:640]),
        local(up_kv.at[:, 1], u_all.at[x, y, :, :, 640:768]),
    ]
    own_o = [
        local(down_o, p_all.at[x, y]),
        local(up_o, o_all.at[x, y]),
    ]
    pl.semaphore_wait(barrier, len(partners))

    def ring_one(part, own, device):
        return (
            send(part(own), part(own), device(1)),
            send(part(own), part(own), device(-1)),
        )

    def ring_two(first, part_lo, part_hi, own, device):
        first[0].wait_recv()
        first[1].wait_recv()
        before, after = wrap(own - 1), wrap(own + 1)
        return (
            send(part_lo(before), part_lo(before), device(1)),
            send(part_hi(after), part_hi(after), device(-1)),
        )

    def gather_one(pool):
        return (
            ring_one(lambda i: pool.at[i, y, 0:4], x, at_x),
            ring_one(lambda i: pool.at[x, i, 4:8], y, at_y),
        )

    def gather_two(pool, a, b):
        return (
            ring_two(a, lambda i: pool.at[i, y, 0:2], lambda i: pool.at[i, y, 2:4], x, at_x),
            ring_two(b, lambda i: pool.at[x, i, 4:6], lambda i: pool.at[x, i, 6:8], y, at_y),
        )

    def gather_three(pool):
        return (
            ring_one(lambda i: pool.at[:, i, 0:4], y, at_y),
            ring_one(lambda i: pool.at[i, :, 4:8], x, at_x),
        )

    def gather_four(pool, a, b):
        return (
            ring_two(a, lambda i: pool.at[:, i, 0:2], lambda i: pool.at[:, i, 2:4], y, at_y),
            ring_two(b, lambda i: pool.at[i, :, 4:6], lambda i: pool.at[i, :, 6:8], x, at_x),
        )

    def landed(copies):
        for copy in copies:
            copy.wait_recv()

    for copy in own_h:
        copy.wait()
    ha1 = ring_one(lambda i: h_a.at[i], x, at_x)
    hb1 = ring_one(lambda i: h_b.at[i], y, at_y)
    z1 = ring_one(lambda i: z_all.at[i * 2 + c], z, at_z)
    s0 = send(z_all.at[t], z_all.at[t], sibling)
    for copy in own_d:
        copy.wait()
    da1 = ring_one(lambda i: d_a.at[i], y, at_y)
    db1 = ring_one(lambda i: d_b.at[i], x, at_x)

    w_copies = []
    for d in range(8):
        i = lax.rem(t + d, 8)
        w_copies.append(local(query_w.at[i], w_all.at[i, :, 0:512]))
        w_copies.append(local(kv_w.at[0, i], w_all.at[i, :, 512:640]))
        w_copies.append(local(kv_w.at[1, i], w_all.at[i, :, 640:768]))
    k_copy = local(keys, k_all)
    v_copy = local(values, v_all)
    o_copies = []
    for d in (2, 1, 3, 0):
        for core in (other, c):
            i = wrap(z + d) * 2 + core
            columns = pl.ds(pl.multiple_of(i * 1024, 1024), 1024)
            o_copies.append(local(out_w.at[:, columns], w_out.at[i]))

    for copy in own_u:
        copy.wait()
    ua1, ub1 = gather_one(u_all)

    ha2 = ring_two(ha1, lambda i: h_a.at[i, 0:80], lambda i: h_a.at[i, 80:144], x, at_x)
    hb2 = ring_two(hb1, lambda i: h_b.at[i, 0:80], lambda i: h_b.at[i, 80:144], y, at_y)
    z2 = ring_two(
        z1, lambda i: z_all.at[i * 2 + c, 0:64], lambda i: z_all.at[i * 2 + c, 64:128], z, at_z
    )
    up_z, down_z = wrap(z + 1), wrap(z - 1)
    s1 = send(z_all.at[up_z * 2 + c], z_all.at[up_z * 2 + c], sibling)
    s2 = send(z_all.at[down_z * 2 + c], z_all.at[down_z * 2 + c], sibling)

    for copy in w_copies:
        copy.wait()
    acc[...] = jnp.zeros_like(acc)

    def project(i):
        acc[...] += mm(z_all[i], w_all[i])

    def project_near(i, _):
        project(wrap(z + i + i // 2) * 2 + c)
        return 0

    lax.fori_loop(0, 3, project_near, 0)

    da2 = ring_two(da1, lambda i: d_a.at[i, 0:4], lambda i: d_a.at[i, 4:8], y, at_y)
    db2 = ring_two(db1, lambda i: d_b.at[i, 0:4], lambda i: d_b.at[i, 4:8], x, at_x)
    ua2, ub2 = gather_two(u_all, ua1, ub1)

    landed(z2)
    far = wrap(z + 2) * 2 + c
    s3 = send(z_all.at[far], z_all.at[far], sibling)
    landed((s0, s1, s2))

    def project_far(i, _):
        mine = wrap(z + 2) * 2 + c
        theirs = wrap(z + i + i // 2) * 2 + other
        project(jnp.where(i == 3, mine, theirs))
        return 0

    lax.fori_loop(0, 4, project_far, 0)
    landed((s3,))
    project(wrap(z + 2) * 2 + other)

    landed(ha2)
    landed(hb2)

    def ids_of(h):
        return jnp.concatenate(
            [h[i, 128:144, 0:128].astype(F32)[0:1] for i in range(4)], axis=1
        )

    def fold(h, d, ids, j, owner, total):
        rows = h[:, 0:128, :].reshape(512, 512)
        maps = d[j].reshape(384, 512)
        every = lax.dot_general(maps, rows, NT, preferred_element_type=F32)
        every = every.reshape(8, 48, 512)
        first = (owner * 8).astype(F32)
        for i in range(8):
            total = total + jnp.where(ids == first + float(i), every[i], 0.0)
        return total

    ids_a, ids_b = ids_of(h_a), ids_of(h_b)
    zero_low = jnp.zeros((48, 512), F32)

    def near_a(i, total):
        j = wrap(y + i + i // 2)
        return fold(h_a, d_a, ids_a, j, x * 4 + j, total)

    def near_b(i, total):
        j = wrap(x + i + i // 2)
        return fold(h_b, d_b, ids_b, j, j * 4 + y, total)

    low_a = lax.fori_loop(0, 3, near_a, zero_low)
    low_b = lax.fori_loop(0, 3, near_b, zero_low)
    landed(da2)
    low_a = fold(h_a, d_a, ids_a, wrap(y + 2), x * 4 + wrap(y + 2), low_a)
    for i in range(4):
        low_send_a[i] = low_a[:, i * 128 : (i + 1) * 128]
    back_a = [
        send(low_send_a.at[wrap(x + d)], low_recv_a.at[x], at_x(d)) for d in (1, 3, 2)
    ]
    landed(db2)
    low_b = fold(h_b, d_b, ids_b, wrap(x + 2), wrap(x + 2) * 4 + y, low_b)
    for i in range(4):
        low_send_b[i] = low_b[:, i * 128 : (i + 1) * 128]
    back_b = [
        send(low_send_b.at[wrap(y + d)], low_recv_b.at[y], at_y(d)) for d in (1, 3, 2)
    ]

    landed(ua2 + ub2)
    ua3, ub3 = gather_three(u_all)

    landed(back_a)
    landed(back_b)
    part = low_send_a[x] + low_send_b[y]
    for d in (1, 2, 3):
        part = part + low_recv_a[wrap(x + d)] + low_recv_b[wrap(y + d)]
    low_parts[t] = part
    over_t = [
        send(low_parts.at[t], low_parts.at[t], (replica, lax.rem(t + d, 8)))
        for d in range(1, 8)
    ]
    for copy in own_o:
        copy.wait()
    pa1, pb1 = gather_one(p_all)
    oa1, ob1 = gather_one(o_all)
    landed(over_t)

    def spread(low, first):
        source = lax.broadcasted_iota(jnp.int32, (128, 128), 0)
        target = lax.broadcasted_iota(jnp.int32, (128, 128), 1)
        pattern = (source == first + lax.rem(target, 16)).astype(BF16)
        return mm(low, pattern)

    owner_ids = ids_col[...]
    lane_adapter = lax.broadcasted_iota(jnp.int32, (128, 128), 1) // 16

    def expand(tiled):
        return jnp.concatenate(
            [
                jnp.where(owner_ids == lane_adapter + 8 * i, tiled, 0.0).astype(BF16)
                for i in range(16)
            ],
            axis=1,
        )

    low = low_parts[0]
    for i in range(1, 8):
        low = low + low_parts[i]
    low = jnp.concatenate([low, jnp.zeros((80, 128), F32)], axis=0)
    low = jnp.transpose(low, (1, 0)).astype(BF16)

    ua4, ub4 = gather_four(u_all, ua3, ub3)
    expand_q = expand(spread(low, 0))
    expand_k = expand(spread(low, 16))
    expand_v = expand(spread(low, 32))
    landed(ua4 + ub4)

    pa2, pb2 = gather_two(p_all, pa1, pb1)
    oa2, ob2 = gather_two(o_all, oa1, ob1)

    def raised(expanded, maps, lo, hi):
        return mm(expanded, maps[:, :, :, :, lo:hi].reshape(2048, hi - lo))

    acc[:, 0:512] += ADAPTER_SCALE * raised(expand_q, u_all, 0, 512)
    acc[:, 512:640] += ADAPTER_SCALE * raised(expand_k, u_all, 512, 640)
    acc[:, 640:768] += ADAPTER_SCALE * raised(expand_v, u_all, 640, 768)

    landed(pa2 + pb2)
    pa3, pb3 = gather_three(p_all)
    landed(oa2 + ob2)

    def rotated(columns):
        flat = acc[:, columns * 128 : (columns + 1) * 128]
        turned = flat * cosines[...] + pltpu.roll(flat, 64, 1) * sines[...]
        return turned.astype(BF16).astype(F32)

    new_key = rotated(4)
    new_value = acc[:, 640:768].astype(BF16).astype(F32)
    row_lengths = jnp.broadcast_to(lengths[...], (128, 128))
    for i in range(8):
        rows = pl.ds(i, 128, stride=8)
        q_rows[rows, :] = rotated(i % 4)
        key_rows[rows, :] = new_key
        value_rows[rows, :] = new_value
        length_rows[rows, :] = row_lengths

    k_copy.wait()
    v_copy.wait()
    scale = 1.0 / (128.0 ** 0.5)

    def attend(b, _):
        first = pl.multiple_of(b * 128, 128)
        rows = pl.ds(first, 128)
        q = q_rows[rows, :]
        q16 = q.astype(BF16)
        scores = []
        for i in range(16):
            scores.append(
                lax.dot_general(
                    q16[i * 8 : (i + 1) * 8], k_all[b * 16 + i], NT, preferred_element_type=F32
                )
            )
        scores = jnp.concatenate(scores, axis=0) * scale
        self_score = jnp.sum(q * key_rows[rows, :], axis=1, keepdims=True) * scale
        slot = lax.broadcasted_iota(jnp.int32, (128, 128), 1).astype(F32)
        valid = slot < length_rows[rows, :]
        highest = jnp.maximum(
            jnp.max(jnp.where(valid, scores, NEGATIVE), axis=1, keepdims=True), self_score
        )
        weights = jnp.where(valid, jnp.exp(scores - highest), 0.0)
        self_weight = jnp.exp(self_score - highest)
        total = jnp.sum(weights, axis=1, keepdims=True) + self_weight
        weights16 = (weights / total).astype(BF16)
        self16 = (self_weight / total).astype(BF16).astype(F32)
        mixed = []
        for i in range(16):
            mixed.append(mm(weights16[i * 8 : (i + 1) * 8], v_all[b * 16 + i]))
        mixed_rows[rows, :] = jnp.concatenate(mixed, axis=0) + self16 * value_rows[rows, :]
        return 0

    lax.fori_loop(0, 8, attend, 0)
    attended = jnp.concatenate(
        [mixed_rows[pl.ds(i, 128, stride=8), :].astype(BF16) for i in range(4)], axis=1
    )

    pa4, pb4 = gather_four(p_all, pa3, pb3)
    oa3, ob3 = gather_three(o_all)
    landed(pa4 + pb4)
    own_ids = h_a[x, 128:144, 0:128].astype(F32)[0:1]
    low_out = jnp.zeros((16, 128), F32)
    for j in range(4):
        maps = p_all[j].reshape(512, 512)
        every = lax.dot_general(maps, attended, NT, preferred_element_type=F32)
        every = every.reshape(32, 16, 128)
        for i in range(32):
            low_out = low_out + jnp.where(own_ids == float(j * 32 + i), every[i], 0.0)
    out_parts[t] = low_out
    out_over_t = [
        send(out_parts.at[t], out_parts.at[t], (replica, lax.rem(t + d, 8)))
        for d in range(1, 8)
    ]

    for copy in o_copies:
        copy.wait()
    to_sibling = {}
    for d in (2, 1, 3, 0):
        i = wrap(z + d)
        sib_send[i] = mm(attended, w_out[i * 2 + other]).astype(BF16)
        to_sibling[d] = send(sib_send.at[i], sib_recv.at[i], sibling)

    def chip_sum(d):
        i = wrap(z + d)
        mine = mm(attended, w_out[i * 2 + c])
        to_sibling[d].wait_recv()
        return mine + sib_recv[i].astype(F32)

    far_send[...] = chip_sum(2).astype(BF16)
    f1 = send(far_send.at[0:64], far_plus, at_z(1))
    f2 = send(far_send.at[64:128], far_minus, at_z(-1))
    total = chip_sum(1)
    f1.wait_recv()
    near_send[0, 0:64] = (total[0:64] + far_plus[...].astype(F32)).astype(BF16)
    near_send[0, 64:128] = total[64:128].astype(BF16)
    n1 = send(near_send.at[0], near_recv.at[0], at_z(1))
    total = chip_sum(3)
    f2.wait_recv()
    near_send[1, 0:64] = total[0:64].astype(BF16)
    near_send[1, 64:128] = (total[64:128] + far_minus[...].astype(F32)).astype(BF16)
    n2 = send(near_send.at[1], near_recv.at[1], at_z(-1))
    own_sum[...] = chip_sum(0)

    landed(out_over_t)
    low_out = out_parts[0]
    for i in range(1, 8):
        low_out = low_out + out_parts[i]
    low_out = jnp.concatenate([low_out, jnp.zeros((112, 128), F32)], axis=0)
    low_out = jnp.transpose(low_out, (1, 0)).astype(BF16)
    expand_o = expand(spread(low_out, 0))
    oa4, ob4 = gather_four(o_all, oa3, ob3)
    landed((n1, n2))
    own_sum[...] += near_recv[0].astype(F32) + near_recv[1].astype(F32)
    landed(oa4 + ob4)
    out[...] = (own_sum[...] + ADAPTER_SCALE * mm(expand_o, o_all[...].reshape(2048, 1024))).astype(BF16)

    for copy in sent:
        copy.wait_send()


def shards(
    hidden,
    query_weight,
    keyvalue_weight,
    output_weight,
    adapter_down_maps,
    adapter_up_query,
    adapter_up_keyvalue,
    adapter_down_output,
    adapter_up_output,
    cached_keys,
    cached_values,
    context_lengths,
    request_list_slots,
    group_adapter_lists,
):
    group = lax.axis_index("replica")
    wanted = lax.dynamic_index_in_dim(group_adapter_lists, group, 0, keepdims=False)
    chosen = request_list_slots[:, None] == jnp.arange(wanted.shape[0], dtype=jnp.int32)[None, :]
    ids = jnp.sum(jnp.where(chosen, wanted[None, :], 0), axis=1)
    ids_rows = jnp.broadcast_to(jnp.tile(ids, 4)[None, :], (16, 512)).astype(BF16)
    half_size = 64
    frequency = ROPE_BASE ** (-(jnp.arange(half_size, dtype=F32) * 2.0) / 128)
    angles = context_lengths.astype(F32)[:, None] * frequency[None, :]
    cosine, sine = jnp.cos(angles), jnp.sin(angles)
    cosines = jnp.concatenate([cosine, cosine], axis=1)
    sines = jnp.concatenate([-sine, sine], axis=1)
    lengths = context_lengths.astype(F32)[:, None]

    hbm = pl.BlockSpec(memory_space=pl.ANY)
    vmem = pl.BlockSpec(memory_space=pltpu.VMEM)
    return pl.pallas_call(
        kernel,
        out_shape=jax.ShapeDtypeStruct((128, 1024), BF16),
        in_specs=[hbm, hbm, vmem, vmem, vmem, vmem] + [hbm] * 10,
        out_specs=vmem,
        scratch_shapes=[
            pltpu.VMEM((8, 128, 1024), BF16),
            pltpu.VMEM((4, 144, 512), BF16),
            pltpu.VMEM((4, 144, 512), BF16),
            pltpu.VMEM((4, 8, 48, 512), BF16),
            pltpu.VMEM((4, 8, 48, 512), BF16),
            pltpu.VMEM((4, 4, 8, 16, 768), BF16),
            pltpu.VMEM((4, 4, 8, 16, 512), BF16),
            pltpu.VMEM((4, 4, 8, 16, 1024), BF16),
            pltpu.VMEM((8, 1024, 768), BF16),
            pltpu.VMEM((8, 512, 1024), BF16),
            pltpu.VMEM((128, 128, 128), BF16),
            pltpu.VMEM((128, 128, 128), BF16),
            pltpu.VMEM((128, 768), F32),
            pltpu.VMEM((4, 48, 128), F32),
            pltpu.VMEM((4, 48, 128), F32),
            pltpu.VMEM((4, 48, 128), F32),
            pltpu.VMEM((4, 48, 128), F32),
            pltpu.VMEM((8, 48, 128), F32),
            pltpu.VMEM((8, 16, 128), F32),
            pltpu.VMEM((1024, 128), F32),
            pltpu.VMEM((1024, 128), F32),
            pltpu.VMEM((1024, 128), F32),
            pltpu.VMEM((1024, 128), F32),
            pltpu.VMEM((1024, 128), F32),
            pltpu.VMEM((4, 128, 1024), BF16),
            pltpu.VMEM((4, 128, 1024), BF16),
            pltpu.VMEM((128, 1024), BF16),
            pltpu.VMEM((64, 1024), BF16),
            pltpu.VMEM((64, 1024), BF16),
            pltpu.VMEM((2, 128, 1024), BF16),
            pltpu.VMEM((2, 128, 1024), BF16),
            pltpu.VMEM((128, 1024), F32),
            pltpu.SemaphoreType.DMA((SENDS,)),
            pltpu.SemaphoreType.DMA((SENDS,)),
            pltpu.SemaphoreType.DMA((LOCALS,)),
        ],
        compiler_params=pltpu.CompilerParams(
            collective_id=0, has_side_effects=True, vmem_limit_bytes=62 * 1024 * 1024
        ),
        cost_estimate=pl.CostEstimate(flops=8_000_000_000, bytes_accessed=32_000_000, transcendentals=0),
    )(
        hidden,
        ids_rows,
        ids[:, None],
        cosines,
        sines,
        lengths,
        query_weight.reshape(8, 1024, 512),
        keyvalue_weight.reshape(2, 8, 1024, 128),
        output_weight,
        jnp.transpose(adapter_down_maps, (0, 2, 1)),
        adapter_up_query,
        adapter_up_keyvalue,
        jnp.transpose(adapter_down_output, (0, 2, 1)),
        adapter_up_output,
        cached_keys.reshape(128, 128, 128),
        cached_values.reshape(128, 128, 128),
    )


def solution(mesh):
    in_specs = (
        P("replica", "tensor"),
        P(None, "tensor"),
        P(None, None, "tensor"),
        P("tensor", None),
        P("replica", "tensor", None),
        P("replica", None, "tensor"),
        P("replica", None, None, "tensor"),
        P("replica", "tensor", None),
        P("replica", None, "tensor"),
        P("replica", "tensor", None, None),
        P("replica", "tensor", None, None),
        P("replica"),
        P("replica"),
        P(),
    )
    out_specs = P("replica", "tensor")
    return jax.shard_map(shards, mesh=mesh, in_specs=in_specs, out_specs=out_specs, check_vma=False)
```

time: 369 us -> 96 us (0.26)
  waiting for transfers between devices: 257 us -> 0 us
  Pallas kernels: 0 us -> 88.5 us
  blocking collectives: 41.7 us -> 0 us
  matrix products: 31.5 us -> 0 us
  between operations: 13.8 us -> 0.02 us
  local copies, waits for them, and re-layouts: 17.1 us -> 4.44 us
  other arithmetic: 7.1 us -> 2.49 us
    all_gather x6 -> x0, waiting for transfers between devices: 232 us -> none  [the longest x1 88.4 us: shards(): lax.all_gather(adapter_down_maps, 'replica', axis=0, tiled=True)]
    pallas_call x0 -> x1, Pallas kernels: none -> 88.5 us  [shards(): pl.pallas_call(kernel, out_shape=jax.ShapeDtypeStruct((128, 1024), BF16),...]
    psum x2 -> x0, blocking collectives: 41.7 us -> none  [the longest x1 26.5 us: shards(): reduced_rows = lax.psum(part_rank, 'tensor').astype(jnp.bfloat16)]
    dot_general x10 -> x0, matrix products: 31.5 us -> none  [the longest x1 6.59 us: shards(): jnp.dot(attention_output, output_weight, preferred_element_type=jnp.float32)]
    reduce_scatter x1 -> x0, waiting for transfers between devices: 21.5 us -> none  [shards(): lax.psum_scatter(partial_value, 'tensor', scatter_dimension=1, tiled=True)]
    gather x5 -> x0, local copies, waits for them, and re-layouts: 16.2 us -> none  [shards(): jnp.take(member, wanted, axis=0)]
  transfers between devices with their start and end apart: 7 -> 0, of which waited for: 6 -> 0; matrix products, arithmetic and copies ran while one was open for 14% -> 0% of each run, Pallas kernels for 0% -> 0%
where the time goes in v1:
time: 96 us; the launch traced here: 95.4 us
  Pallas kernels  88.5 us (92%)
  local copies, waits for them, and re-layouts  4.44 us (5%)
  other arithmetic  2.49 us (3%)
    pallas_call x1, Pallas kernels, shards(): pl.pallas_call(kernel, out_shape=jax.ShapeDtypeStruct((128, 1024), BF16),...  88.5 us
    unnamed x3, local copies, waits for them, and re-layouts  2.37 us

profile of v1, /device:TPU:0, one launch (start us, length us, event | category | flops | bytes accessed | tf_op | source)
XLA Modules:
  0.0 95.4 jit_solution(10832212649571932623)
XLA Ops:
  0.0 0.0 copy-start
  0.0 0.7 copy-done
  0.7 0.7 select_reduce_fusion
  1.5 0.7 convert_bitcast_fusion
  2.1 0.6 broadcast_in_dim.33.ids_rows
  2.7 0.7 copy.18.lengths
  3.5 0.7 copy.17.ids_col
  4.2 0.3 fusion
  4.5 0.8 pad_maximum_fusion
  5.3 88.5 %shard_map.136 = bf16[128,1024]{1,0:T(8,128)(2,1)} custom-call(bf16[128,1024]{1,0:T(8,128)(2,1)} %hidden.1, bf16[16,512]{1,0:T(8,128)(2,1)} %broadcast_in_dim.33.ids_rows, s32[128,1]{1,0:T(8,128)} %copy.17.ids_col, f32[128,128]{1,0:T(8,128)} %get-tuple-element.10.cosines, f32[128,128]{1,0:T(8,128)} %get-tuple-element.11.sines, f32[128,1]{1,0:T(8,128)} %copy.18.lengths, ...), custom_call_target="tpu_custom_call" | custom-call | flops 8000000000 | bytes 32000000 | tf_op jit(solution)/shard_map/pallas_call | solution.py:475
  93.7 1.7 %copy.20 = bf16[128,1024]{1,0:T(8,128)(2,1)} copy(bf16[128,1024]{1,0:T(8,128)(2,1)} %shard_map.136) | data formatting | bytes 524288
  (4 shorter events, 0.0 us)
Async XLA Ops:
  0.0 0.7 copy-start

commit v2 on v1

--- a/solution.py
+++ b/solution.py
@@ -2,6 +2,7 @@
 
 import jax
 import jax.numpy as jnp
+import numpy as np
 from jax import lax
 from jax.experimental import pallas as pl
 from jax.experimental.pallas import tpu as pltpu
@@ -14,8 +15,8 @@
 F32 = jnp.float32
 NT = (((1,), (1,)), ((), ()))
 NEGATIVE = -1e30
-SENDS = 104
-LOCALS = 56
+SENDS = 144
+LOCALS = 64
 
 
 def mm(a, b):
@@ -23,13 +24,14 @@
 
 
 def kernel(
-    hidden, ids_rows, ids_col, cosines, sines, lengths,
+    hidden, lists, slots, lengths, frequencies,
     query_w, kv_w, out_w, down, up_q, up_kv, down_o, up_o, keys, values,
     out,
-    z_all, h_a, h_b, d_a, d_b, u_all, p_all, o_all, w_all, w_out, k_all, v_all,
+    z_all, h_a, h_b, d_a, d_b, u_all, p_all, o_a, o_b, w_all, w_out, k_all, v_all,
     acc, low_send_a, low_recv_a, low_send_b, low_recv_b, low_parts, out_parts,
     q_rows, key_rows, value_rows, length_rows, mixed_rows,
-    sib_send, sib_recv, far_send, far_plus, far_minus, near_send, near_recv, own_sum,
+    sib_send, sib_recv, own_sum, lists_v, slots_v, lengths_v, frequencies_v, id_columns_a, id_columns_b,
+    low_a, low_b, z_far, z_half, z_near, z_back, x_far, x_half, x_near, x_back, y_far, y_half, y_near, y_back,
     send_sem, recv_sem, local_sem,
 ):
     replica = lax.axis_index("replica")
@@ -79,12 +81,11 @@
     for partner in partners:
         pl.semaphore_signal(barrier, inc=1, device_id=partner, device_id_type=MESH)
 
+    own_small = [local(lists, lists_v), local(slots, slots_v)]
     own_h = [
+        local(hidden.at[:, 0:512], h_a.at[x, 0:128]),
+        local(hidden.at[:, 512:1024], h_b.at[y, 0:128]),
         local(hidden, z_all.at[t]),
-        local(hidden.at[:, 0:512], h_a.at[x, 0:128]),
-        local(ids_rows, h_a.at[x, 128:144]),
-        local(hidden.at[:, 512:1024], h_b.at[y, 0:128]),
-        local(ids_rows, h_b.at[y, 128:144]),
     ]
     own_d = [
         local(down.at[:, :, 0:512], d_a.at[y]),
@@ -95,65 +96,89 @@
         local(up_kv.at[:, 0], u_all.at[x, y, :, :, 512:640]),
         local(up_kv.at[:, 1], u_all.at[x, y, :, :, 640:768]),
     ]
+    own_p = local(down_o, p_all.at[x, y])
     own_o = [
-        local(down_o, p_all.at[x, y]),
-        local(up_o, o_all.at[x, y]),
-    ]
+        local(up_o.at[:, :, 0:512], o_a.at[y]),
+        local(up_o.at[:, :, 512:1024], o_b.at[x]),
+    ]
+    own_late = [local(lengths, lengths_v), local(frequencies, frequencies_v)]
+
+    for copy in own_small:
+        copy.wait()
+    wanted = lists_v[pl.ds(replica, 1), :].astype(F32).astype(BF16)
+    picked = lax.broadcasted_iota(jnp.int32, (32, 128), 0) == slots_v[...]
+    own_ids = mm(jnp.broadcast_to(wanted, (16, 32)), picked.astype(F32).astype(BF16))
+    id_rows = jnp.concatenate([own_ids] * 4, axis=1).astype(BF16)
+    for copy in own_h:
+        copy.wait()
+    h_a[x, 128:144, :] = id_rows
+    h_b[y, 128:144, :] = id_rows
     pl.semaphore_wait(barrier, len(partners))
 
-    def ring_one(part, own, device):
-        return (
-            send(part(own), part(own), device(1)),
-            send(part(own), part(own), device(-1)),
-        )
-
-    def ring_two(first, part_lo, part_hi, own, device):
-        first[0].wait_recv()
-        first[1].wait_recv()
-        before, after = wrap(own - 1), wrap(own + 1)
-        return (
-            send(part_lo(before), part_lo(before), device(1)),
-            send(part_hi(after), part_hi(after), device(-1)),
-        )
-
-    def gather_one(pool):
-        return (
-            ring_one(lambda i: pool.at[i, y, 0:4], x, at_x),
-            ring_one(lambda i: pool.at[x, i, 4:8], y, at_y),
-        )
-
-    def gather_two(pool, a, b):
-        return (
-            ring_two(a, lambda i: pool.at[i, y, 0:2], lambda i: pool.at[i, y, 2:4], x, at_x),
-            ring_two(b, lambda i: pool.at[x, i, 4:6], lambda i: pool.at[x, i, 6:8], y, at_y),
-        )
-
-    def gather_three(pool):
-        return (
-            ring_one(lambda i: pool.at[:, i, 0:4], y, at_y),
-            ring_one(lambda i: pool.at[i, :, 4:8], x, at_x),
-        )
-
-    def gather_four(pool, a, b):
-        return (
-            ring_two(a, lambda i: pool.at[:, i, 0:2], lambda i: pool.at[:, i, 2:4], y, at_y),
-            ring_two(b, lambda i: pool.at[i, :, 4:6], lambda i: pool.at[i, :, 6:8], x, at_x),
-        )
+    arrived = set()
 
     def landed(copies):
         for copy in copies:
-            copy.wait_recv()
-
-    for copy in own_h:
-        copy.wait()
-    ha1 = ring_one(lambda i: h_a.at[i], x, at_x)
-    hb1 = ring_one(lambda i: h_b.at[i], y, at_y)
-    z1 = ring_one(lambda i: z_all.at[i * 2 + c], z, at_z)
+            if id(copy) not in arrived:
+                arrived.add(id(copy))
+                copy.wait_recv()
+
+    def ring_one(lo, hi, own, device):
+        return [
+            send(lo(own), lo(own), device(1)),
+            send(hi(own), hi(own), device(-1)),
+            send(hi(own), hi(own), device(1)),
+            send(lo(own), lo(own), device(-1)),
+        ]
+
+    def ring_two(first, lo, hi, own, device):
+        before, after = wrap(own - 1), wrap(own + 1)
+        landed(first[0:1])
+        onward = [send(lo(before), lo(before), device(1))]
+        landed(first[1:2])
+        onward.append(send(hi(after), hi(after), device(-1)))
+        return first + onward
+
+    def pool_parts(pool):
+        return (
+            (lambda i: pool.at[i, y, 0:2], lambda i: pool.at[i, y, 2:4], x, at_x),
+            (lambda i: pool.at[x, i, 4:6], lambda i: pool.at[x, i, 6:8], y, at_y),
+            (lambda i: pool.at[:, i, 0:2], lambda i: pool.at[:, i, 2:4], y, at_y),
+            (lambda i: pool.at[i, :, 4:6], lambda i: pool.at[i, :, 6:8], x, at_x),
+        )
+
+    def gather_one(pool):
+        parts = pool_parts(pool)
+        return ring_one(*parts[0]), ring_one(*parts[1])
+
+    def gather_two(pool, a, b):
+        parts = pool_parts(pool)
+        return ring_two(a, *parts[0]), ring_two(b, *parts[1])
+
+    def gather_three(pool):
+        parts = pool_parts(pool)
+        return ring_one(*parts[2]), ring_one(*parts[3])
+
+    def gather_four(pool, a, b):
+        parts = pool_parts(pool)
+        return ring_two(a, *parts[2]), ring_two(b, *parts[3])
+
+    ha_parts = (lambda i: h_a.at[i, 0:80], lambda i: h_a.at[i, 80:144], x, at_x)
+    hb_parts = (lambda i: h_b.at[i, 0:80], lambda i: h_b.at[i, 80:144], y, at_y)
+    z_parts = (lambda i: z_all.at[i * 2 + c, 0:64], lambda i: z_all.at[i * 2 + c, 64:128], z, at_z)
+    da_parts = (lambda i: d_a.at[i, 0:4], lambda i: d_a.at[i, 4:8], y, at_y)
+    db_parts = (lambda i: d_b.at[i, 0:4], lambda i: d_b.at[i, 4:8], x, at_x)
+    oa_parts = (lambda i: o_a.at[i, 0:4], lambda i: o_a.at[i, 4:8], y, at_y)
+    ob_parts = (lambda i: o_b.at[i, 0:4], lambda i: o_b.at[i, 4:8], x, at_x)
+
+    ha1 = ring_one(*ha_parts)
+    hb1 = ring_one(*hb_parts)
+    z1 = ring_one(*z_parts)
     s0 = send(z_all.at[t], z_all.at[t], sibling)
     for copy in own_d:
         copy.wait()
-    da1 = ring_one(lambda i: d_a.at[i], y, at_y)
-    db1 = ring_one(lambda i: d_b.at[i], x, at_x)
+    da1 = ring_one(*da_parts)
+    db1 = ring_one(*db_parts)
 
     w_copies = []
     for d in range(8):
@@ -174,11 +199,10 @@
         copy.wait()
     ua1, ub1 = gather_one(u_all)
 
-    ha2 = ring_two(ha1, lambda i: h_a.at[i, 0:80], lambda i: h_a.at[i, 80:144], x, at_x)
-    hb2 = ring_two(hb1, lambda i: h_b.at[i, 0:80], lambda i: h_b.at[i, 80:144], y, at_y)
-    z2 = ring_two(
-        z1, lambda i: z_all.at[i * 2 + c, 0:64], lambda i: z_all.at[i * 2 + c, 64:128], z, at_z
-    )
+    ha2 = ring_two(ha1, *ha_parts)
+    hb2 = ring_two(hb1, *hb_parts)
+    z2 = ring_two(z1, *z_parts)
+    landed(z1)
     up_z, down_z = wrap(z + 1), wrap(z - 1)
     s1 = send(z_all.at[up_z * 2 + c], z_all.at[up_z * 2 + c], sibling)
     s2 = send(z_all.at[down_z * 2 + c], z_all.at[down_z * 2 + c], sibling)
@@ -196,8 +220,21 @@
 
     lax.fori_loop(0, 3, project_near, 0)
 
-    da2 = ring_two(da1, lambda i: d_a.at[i, 0:4], lambda i: d_a.at[i, 4:8], y, at_y)
-    db2 = ring_two(db1, lambda i: d_b.at[i, 0:4], lambda i: d_b.at[i, 4:8], x, at_x)
+    for copy in own_late:
+        copy.wait()
+
+    def column(row):
+        return jnp.transpose(jnp.broadcast_to(row, (128, 128)), (1, 0))
+
+    row_lengths = column(lengths_v[...].astype(F32))
+    angles = row_lengths * frequencies_v[...]
+    lane = lax.broadcasted_iota(jnp.int32, (128, 128), 1)
+    cosines = jnp.cos(angles)
+    sines = jnp.where(lane < 64, -jnp.sin(angles), jnp.sin(angles))
+    owner_ids = column(own_ids[0:1])
+
+    da2 = ring_two(da1, *da_parts)
+    db2 = ring_two(db1, *db_parts)
     ua2, ub2 = gather_two(u_all, ua1, ub1)
 
     landed(z2)
@@ -234,6 +271,11 @@
         return total
 
     ids_a, ids_b = ids_of(h_a), ids_of(h_b)
+    for i in range(4):
+        id_columns_a[i] = column(ids_a[:, i * 128 : (i + 1) * 128])
+        id_columns_b[i] = column(ids_b[:, i * 128 : (i + 1) * 128])
+    landed(da1)
+    landed(db1)
     zero_low = jnp.zeros((48, 512), F32)
 
     def near_a(i, total):
@@ -244,19 +286,19 @@
         j = wrap(x + i + i // 2)
         return fold(h_b, d_b, ids_b, j, j * 4 + y, total)
 
-    low_a = lax.fori_loop(0, 3, near_a, zero_low)
-    low_b = lax.fori_loop(0, 3, near_b, zero_low)
+    sum_a = lax.fori_loop(0, 3, near_a, zero_low)
+    sum_b = lax.fori_loop(0, 3, near_b, zero_low)
     landed(da2)
-    low_a = fold(h_a, d_a, ids_a, wrap(y + 2), x * 4 + wrap(y + 2), low_a)
+    sum_a = fold(h_a, d_a, ids_a, wrap(y + 2), x * 4 + wrap(y + 2), sum_a)
     for i in range(4):
-        low_send_a[i] = low_a[:, i * 128 : (i + 1) * 128]
+        low_send_a[i] = sum_a[:, i * 128 : (i + 1) * 128]
     back_a = [
         send(low_send_a.at[wrap(x + d)], low_recv_a.at[x], at_x(d)) for d in (1, 3, 2)
     ]
     landed(db2)
-    low_b = fold(h_b, d_b, ids_b, wrap(x + 2), wrap(x + 2) * 4 + y, low_b)
+    sum_b = fold(h_b, d_b, ids_b, wrap(x + 2), wrap(x + 2) * 4 + y, sum_b)
     for i in range(4):
-        low_send_b[i] = low_b[:, i * 128 : (i + 1) * 128]
+        low_send_b[i] = sum_b[:, i * 128 : (i + 1) * 128]
     back_b = [
         send(low_send_b.at[wrap(y + d)], low_recv_b.at[y], at_y(d)) for d in (1, 3, 2)
     ]
@@ -274,10 +316,8 @@
         send(low_parts.at[t], low_parts.at[t], (replica, lax.rem(t + d, 8)))
         for d in range(1, 8)
     ]
-    for copy in own_o:
-        copy.wait()
+    own_p.wait()
     pa1, pb1 = gather_one(p_all)
-    oa1, ob1 = gather_one(o_all)
     landed(over_t)
 
     def spread(low, first):
@@ -286,13 +326,12 @@
         pattern = (source == first + lax.rem(target, 16)).astype(BF16)
         return mm(low, pattern)
 
-    owner_ids = ids_col[...]
-    lane_adapter = lax.broadcasted_iota(jnp.int32, (128, 128), 1) // 16
+    lane_adapter = (lane // 16).astype(F32)
 
     def expand(tiled):
         return jnp.concatenate(
             [
-                jnp.where(owner_ids == lane_adapter + 8 * i, tiled, 0.0).astype(BF16)
+                jnp.where(owner_ids == lane_adapter + 8.0 * i, tiled, 0.0).astype(BF16)
                 for i in range(16)
             ],
             axis=1,
@@ -308,10 +347,15 @@
     expand_q = expand(spread(low, 0))
     expand_k = expand(spread(low, 16))
     expand_v = expand(spread(low, 32))
+
+    pa2, pb2 = gather_two(p_all, pa1, pb1)
     landed(ua4 + ub4)
-
-    pa2, pb2 = gather_two(p_all, pa1, pb1)
-    oa2, ob2 = gather_two(o_all, oa1, ob1)
+    landed(pa2 + pb2)
+    pa3, pb3 = gather_three(p_all)
+    for copy in own_o:
+        copy.wait()
+    oa1 = ring_one(*oa_parts)
+    ob1 = ring_one(*ob_parts)
 
     def raised(expanded, maps, lo, hi):
         return mm(expanded, maps[:, :, :, :, lo:hi].reshape(2048, hi - lo))
@@ -320,18 +364,13 @@
     acc[:, 512:640] += ADAPTER_SCALE * raised(expand_k, u_all, 512, 640)
     acc[:, 640:768] += ADAPTER_SCALE * raised(expand_v, u_all, 640, 768)
 
-    landed(pa2 + pb2)
-    pa3, pb3 = gather_three(p_all)
-    landed(oa2 + ob2)
-
     def rotated(columns):
         flat = acc[:, columns * 128 : (columns + 1) * 128]
-        turned = flat * cosines[...] + pltpu.roll(flat, 64, 1) * sines[...]
+        turned = flat * cosines + pltpu.roll(flat, 64, 1) * sines
         return turned.astype(BF16).astype(F32)
 
     new_key = rotated(4)
     new_value = acc[:, 640:768].astype(BF16).astype(F32)
-    row_lengths = jnp.broadcast_to(lengths[...], (128, 128))
     for i in range(8):
         rows = pl.ds(i, 128, stride=8)
         q_rows[rows, :] = rotated(i % 4)
@@ -373,22 +412,24 @@
         mixed_rows[rows, :] = jnp.concatenate(mixed, axis=0) + self16 * value_rows[rows, :]
         return 0
 
-    lax.fori_loop(0, 8, attend, 0)
+    lax.fori_loop(0, 4, attend, 0)
+    pa4, pb4 = gather_four(p_all, pa3, pb3)
+    oa2 = ring_two(oa1, *oa_parts)
+    ob2 = ring_two(ob1, *ob_parts)
+    lax.fori_loop(4, 8, attend, 0)
     attended = jnp.concatenate(
         [mixed_rows[pl.ds(i, 128, stride=8), :].astype(BF16) for i in range(4)], axis=1
     )
 
-    pa4, pb4 = gather_four(p_all, pa3, pb3)
-    oa3, ob3 = gather_three(o_all)
     landed(pa4 + pb4)
-    own_ids = h_a[x, 128:144, 0:128].astype(F32)[0:1]
+    own_row = own_ids[0:1]
     low_out = jnp.zeros((16, 128), F32)
     for j in range(4):
         maps = p_all[j].reshape(512, 512)
         every = lax.dot_general(maps, attended, NT, preferred_element_type=F32)
         every = every.reshape(32, 16, 128)
         for i in range(32):
-            low_out = low_out + jnp.where(own_ids == float(j * 32 + i), every[i], 0.0)
+            low_out = low_out + jnp.where(own_row == float(j * 32 + i), every[i], 0.0)
     out_parts[t] = low_out
     out_over_t = [
         send(out_parts.at[t], out_parts.at[t], (replica, lax.rem(t + d, 8)))
@@ -402,27 +443,6 @@
         i = wrap(z + d)
         sib_send[i] = mm(attended, w_out[i * 2 + other]).astype(BF16)
         to_sibling[d] = send(sib_send.at[i], sib_recv.at[i], sibling)
-
-    def chip_sum(d):
-        i = wrap(z + d)
-        mine = mm(attended, w_out[i * 2 + c])
-        to_sibling[d].wait_recv()
-        return mine + sib_recv[i].astype(F32)
-
-    far_send[...] = chip_sum(2).astype(BF16)
-    f1 = send(far_send.at[0:64], far_plus, at_z(1))
-    f2 = send(far_send.at[64:128], far_minus, at_z(-1))
-    total = chip_sum(1)
-    f1.wait_recv()
-    near_send[0, 0:64] = (total[0:64] + far_plus[...].astype(F32)).astype(BF16)
-    near_send[0, 64:128] = total[64:128].astype(BF16)
-    n1 = send(near_send.at[0], near_recv.at[0], at_z(1))
-    total = chip_sum(3)
-    f2.wait_recv()
-    near_send[1, 0:64] = total[0:64].astype(BF16)
-    near_send[1, 64:128] = (total[64:128] + far_minus[...].astype(F32)).astype(BF16)
-    n2 = send(near_send.at[1], near_recv.at[1], at_z(-1))
-    own_sum[...] = chip_sum(0)
 
     landed(out_over_t)
     low_out = out_parts[0]
@@ -430,12 +450,74 @@
         low_out = low_out + out_parts[i]
     low_out = jnp.concatenate([low_out, jnp.zeros((112, 128), F32)], axis=0)
     low_out = jnp.transpose(low_out, (1, 0)).astype(BF16)
-    expand_o = expand(spread(low_out, 0))
-    oa4, ob4 = gather_four(o_all, oa3, ob3)
-    landed((n1, n2))
-    own_sum[...] += near_recv[0].astype(F32) + near_recv[1].astype(F32)
-    landed(oa4 + ob4)
-    out[...] = (own_sum[...] + ADAPTER_SCALE * mm(expand_o, o_all[...].reshape(2048, 1024))).astype(BF16)
+    tiled = spread(low_out, 0).astype(BF16)
+    low_a[x] = tiled
+    low_b[y] = tiled
+    around_a = [send(low_a.at[x], low_a.at[x], at_x(d)) for d in (2, 1, 3)]
+    around_b = [send(low_b.at[y], low_b.at[y], at_y(d)) for d in (2, 1, 3)]
+
+    def sum_far(block, far, half, device):
+        far[...] = block.astype(BF16)
+        return [
+            send(far.at[0:64], half.at[0], device(1)),
+            send(far.at[64:128], half.at[1], device(-1)),
+        ]
+
+    def sum_near(block, d, halves, half, near, back, device):
+        if d == 1:
+            landed(halves[0:1])
+            near[0, 0:64] = (block[0:64] + half[0].astype(F32)).astype(BF16)
+            near[0, 64:128] = block[64:128].astype(BF16)
+            return send(near.at[0], back.at[0], device(1))
+        landed(halves[1:2])
+        near[1, 0:64] = block[0:64].astype(BF16)
+        near[1, 64:128] = (block[64:128] + half[1].astype(F32)).astype(BF16)
+        return send(near.at[1], back.at[1], device(-1))
+
+    def chip_sum(d):
+        i = wrap(z + d)
+        mine = mm(attended, w_out[i * 2 + c])
+        landed([to_sibling[d]])
+        return mine + sib_recv[i].astype(F32)
+
+    halves = sum_far(chip_sum(2), z_far, z_half, at_z)
+    z_plus = sum_near(chip_sum(1), 1, halves, z_half, z_near, z_back, at_z)
+    z_minus = sum_near(chip_sum(3), 3, halves, z_half, z_near, z_back, at_z)
+
+    landed(oa2)
+    landed(ob2)
+    landed(around_a)
+    landed(around_b)
+
+    def product(g, columns, lows, owner, maps):
+        rows = lows[g].astype(F32)
+        blocks = []
+        for j in range(4):
+            first = (owner(j) * 8).astype(F32)
+            blocks.append(jnp.where(columns[g] == lane_adapter + first, rows, 0.0).astype(BF16))
+        return ADAPTER_SCALE * mm(jnp.concatenate(blocks, axis=1), maps[...].reshape(512, 512))
+
+    def product_a(d):
+        return product(wrap(x + d), id_columns_a, low_a, lambda j: x * 4 + j, o_a)
+
+    def product_b(d):
+        return product(wrap(y + d), id_columns_b, low_b, lambda j: j * 4 + y, o_b)
+
+    halves_a = sum_far(product_a(2), x_far, x_half, at_x)
+    halves_b = sum_far(product_b(2), y_far, y_half, at_y)
+    near_plus_a, near_plus_b = product_a(1), product_b(1)
+    x_plus = sum_near(near_plus_a, 1, halves_a, x_half, x_near, x_back, at_x)
+    y_plus = sum_near(near_plus_b, 1, halves_b, y_half, y_near, y_back, at_y)
+    x_minus = sum_near(product_a(3), 3, halves_a, x_half, x_near, x_back, at_x)
+    y_minus = sum_near(product_b(3), 3, halves_b, y_half, y_near, y_back, at_y)
+    own_sum[...] = chip_sum(0)
+    own_sum[:, 0:512] += product_a(0)
+    own_sum[:, 512:1024] += product_b(0)
+    landed([z_plus, z_minus])
+    own_sum[...] += z_back[0].astype(F32) + z_back[1].astype(F32)
+    landed([x_plus, x_minus, y_plus, y_minus])
+    out[:, 0:512] = own_sum[:, 0:512] + (x_back[0].astype(F32) + x_back[1].astype(F32))
+    out[:, 512:1024] = own_sum[:, 512:1024] + (y_back[0].astype(F32) + y_back[1].astype(F32))
 
     for copy in sent:
         copy.wait_send()
@@ -457,25 +539,16 @@
     request_list_slots,
     group_adapter_lists,
 ):
-    group = lax.axis_index("replica")
-    wanted = lax.dynamic_index_in_dim(group_adapter_lists, group, 0, keepdims=False)
-    chosen = request_list_slots[:, None] == jnp.arange(wanted.shape[0], dtype=jnp.int32)[None, :]
-    ids = jnp.sum(jnp.where(chosen, wanted[None, :], 0), axis=1)
-    ids_rows = jnp.broadcast_to(jnp.tile(ids, 4)[None, :], (16, 512)).astype(BF16)
-    half_size = 64
-    frequency = ROPE_BASE ** (-(jnp.arange(half_size, dtype=F32) * 2.0) / 128)
-    angles = context_lengths.astype(F32)[:, None] * frequency[None, :]
-    cosine, sine = jnp.cos(angles), jnp.sin(angles)
-    cosines = jnp.concatenate([cosine, cosine], axis=1)
-    sines = jnp.concatenate([-sine, sine], axis=1)
-    lengths = context_lengths.astype(F32)[:, None]
+    pairs = np.arange(64, dtype=np.float32) * np.float32(2.0) / np.float32(128.0)
+    frequency = np.power(np.float32(ROPE_BASE), -pairs).astype(np.float32)
+    frequencies = jnp.asarray(np.concatenate([frequency, frequency])[None, :])
 
     hbm = pl.BlockSpec(memory_space=pl.ANY)
     vmem = pl.BlockSpec(memory_space=pltpu.VMEM)
-    return pl.pallas_call(
+    result = pl.pallas_call(
         kernel,
-        out_shape=jax.ShapeDtypeStruct((128, 1024), BF16),
-        in_specs=[hbm, hbm, vmem, vmem, vmem, vmem] + [hbm] * 10,
+        out_shape=jax.ShapeDtypeStruct((128, 1024), F32),
+        in_specs=[hbm] * 15,
         out_specs=vmem,
         scratch_shapes=[
             pltpu.VMEM((8, 128, 1024), BF16),
@@ -485,7 +558,8 @@
             pltpu.VMEM((4, 8, 48, 512), BF16),
             pltpu.VMEM((4, 4, 8, 16, 768), BF16),
             pltpu.VMEM((4, 4, 8, 16, 512), BF16),
-            pltpu.VMEM((4, 4, 8, 16, 1024), BF16),
+            pltpu.VMEM((4, 8, 16, 512), BF16),
+            pltpu.VMEM((4, 8, 16, 512), BF16),
             pltpu.VMEM((8, 1024, 768), BF16),
             pltpu.VMEM((8, 512, 1024), BF16),
             pltpu.VMEM((128, 128, 128), BF16),
@@ -504,12 +578,27 @@
             pltpu.VMEM((1024, 128), F32),
             pltpu.VMEM((4, 128, 1024), BF16),
             pltpu.VMEM((4, 128, 1024), BF16),
+            pltpu.VMEM((128, 1024), F32),
+            pltpu.VMEM((16, 32), jnp.int32),
+            pltpu.VMEM((1, 128), jnp.int32),
+            pltpu.VMEM((1, 128), jnp.int32),
+            pltpu.VMEM((1, 128), F32),
+            pltpu.VMEM((4, 128, 128), F32),
+            pltpu.VMEM((4, 128, 128), F32),
+            pltpu.VMEM((4, 128, 128), BF16),
+            pltpu.VMEM((4, 128, 128), BF16),
             pltpu.VMEM((128, 1024), BF16),
-            pltpu.VMEM((64, 1024), BF16),
-            pltpu.VMEM((64, 1024), BF16),
+            pltpu.VMEM((2, 64, 1024), BF16),
             pltpu.VMEM((2, 128, 1024), BF16),
             pltpu.VMEM((2, 128, 1024), BF16),
-            pltpu.VMEM((128, 1024), F32),
+            pltpu.VMEM((128, 512), BF16),
+            pltpu.VMEM((2, 64, 512), BF16),
+            pltpu.VMEM((2, 128, 512), BF16),
+            pltpu.VMEM((2, 128, 512), BF16),
+            pltpu.VMEM((128, 512), BF16),
+            pltpu.VMEM((2, 64, 512), BF16),
+            pltpu.VMEM((2, 128, 512), BF16),
+            pltpu.VMEM((2, 128, 512), BF16),
             pltpu.SemaphoreType.DMA((SENDS,)),
             pltpu.SemaphoreType.DMA((SENDS,)),
             pltpu.SemaphoreType.DMA((LOCALS,)),
@@ -520,11 +609,10 @@
         cost_estimate=pl.CostEstimate(flops=8_000_000_000, bytes_accessed=32_000_000, transcendentals=0),
     )(
         hidden,
-        ids_rows,
-        ids[:, None],
-        cosines,
-        sines,
-        lengths,
+        group_adapter_lists,
+        request_list_slots[None, :],
+        context_lengths[None, :],
+        frequencies,
         query_weight.reshape(8, 1024, 512),
         keyvalue_weight.reshape(2, 8, 1024, 128),
         output_weight,
@@ -536,6 +624,7 @@
         cached_keys.reshape(128, 128, 128),
         cached_values.reshape(128, 128, 128),
     )
+    return result.astype(BF16)
 
 
 def solution(mesh):

time: 96 us -> 86.4 us (0.900)
  local copies, waits for them, and re-layouts: 4.44 us -> 0 us
  Pallas kernels: 88.5 us -> 84.4 us
    pallas_call x1, Pallas kernels: 88.5 us -> 84.4 us  [shards(): pl.pallas_call(kernel, out_shape=jax.ShapeDtypeStruct((128, 1024), F32),...]
    unnamed x3 -> x0, local copies, waits for them, and re-layouts: 2.37 us -> none
    broadcast_in_dim x4 -> x0, local copies, waits for them, and re-layouts: 2.07 us -> none  [the longest x1 0.74 us: shards(): ids[:, None]]
    convert_element_type x1, other arithmetic: 0.01 us -> 1.78 us  [shards(): return result.astype(BF16)]
where the time goes in v2:
time: 86.4 us; the launch traced here: 86.2 us
  Pallas kernels  84.4 us (98%)
  other arithmetic  1.78 us (2%)
    pallas_call x1, Pallas kernels, shards(): pl.pallas_call(kernel, out_shape=jax.ShapeDtypeStruct((128, 1024), F32),...  84.4 us
    convert_element_type x1, other arithmetic, shards(): return result.astype(BF16)  1.78 us

profile of v2, /device:TPU:0, one launch (start us, length us, event | category | flops | bytes accessed | tf_op | source)
XLA Modules:
  0.0 86.2 jit_solution(16907425500604258015)
XLA Ops:
  0.0 84.4 %shard_map.145 = f32[128,1024]{1,0:T(8,128)} custom-call(bf16[128,1024]{1,0:T(8,128)(2,1)} %hidden.1, s32[16,32]{1,0:T(8,128)} %lists.1, s32[1,128]{1,0:T(1,128)} %bitcast.14, s32[1,128]{1,0:T(1,128)} %bitcast.15, f32[1,128]{1,0:T(1,128)} %constant.2.clone.frequencies, bf16[8,1024,512]{2,1,0:T(8,128)(2,1)} %bitcast.8, bf16[2,8,1024,128]{3,2,1,0:T(8,128)(2,1)} %bitcast.9, ...), custom_call_target="tpu_custom_call" | custom-call | flops 8000000000 | bytes 32000000 | tf_op jit(solution)/shard_map/pallas_call | solution.py:548
  84.4 1.8 %convert_element_type.3 = bf16[128,1024]{1,0:T(8,128)(2,1)} convert(f32[128,1024]{1,0:T(8,128)} %shard_map.145) | non-fusion elementwise | flops 131072 | bytes 786432 | tf_op jit(solution)/shard_map/convert_element_type | solution.py:627

commit v3 on v2

--- a/solution.py
+++ b/solution.py
@@ -15,7 +15,7 @@
 F32 = jnp.float32
 NT = (((1,), (1,)), ((), ()))
 NEGATIVE = -1e30
-SENDS = 144
+SENDS = 160
 LOCALS = 64
 
 
@@ -27,13 +27,18 @@
     hidden, lists, slots, lengths, frequencies,
     query_w, kv_w, out_w, down, up_q, up_kv, down_o, up_o, keys, values,
     out,
-    z_all, h_a, h_b, d_a, d_b, u_all, p_all, o_a, o_b, w_all, w_out, k_all, v_all,
+    z_all, h_a, h_b, d_a, d_b, u_a, u_b, p_all, o_a, o_b, w_all, w_out, k_all, v_all,
     acc, low_send_a, low_recv_a, low_send_b, low_recv_b, low_parts, out_parts,
+    low_mine, low_theirs, out_mine, out_theirs,
     q_rows, key_rows, value_rows, length_rows, mixed_rows,
     sib_send, sib_recv, own_sum, lists_v, slots_v, lengths_v, frequencies_v, id_columns_a, id_columns_b,
-    low_a, low_b, z_far, z_half, z_near, z_back, x_far, x_half, x_near, x_back, y_far, y_half, y_near, y_back,
-    send_sem, recv_sem, local_sem,
+    low_a, low_b, out_low_a, out_low_b, *sums,
 ):
+    (
+        z_far, z_half, z_near, z_back, x_far, x_half, x_near, x_back, y_far, y_half, y_near, y_back,
+        xu_far, xu_half, xu_near, xu_back, yu_far, yu_half, yu_near, yu_back,
+        send_sem, recv_sem, local_sem,
+    ) = sums
     replica = lax.axis_index("replica")
     t = lax.axis_index("tensor")
     x, y = replica // 4, replica % 4
@@ -77,7 +82,7 @@
 
     barrier = pltpu.get_barrier_semaphore()
     partners = [at_x(d) for d in (1, 2, 3)] + [at_y(d) for d in (1, 2, 3)]
-    partners += [(replica, lax.rem(t + d, 8)) for d in range(1, 8)]
+    partners += [at_z(d) for d in (1, 2, 3)] + [sibling]
     for partner in partners:
         pl.semaphore_signal(barrier, inc=1, device_id=partner, device_id_type=MESH)
 
@@ -92,9 +97,10 @@
         local(down.at[:, :, 512:1024], d_b.at[x]),
     ]
     own_u = [
-        local(up_q, u_all.at[x, y, :, :, 0:512]),
-        local(up_kv.at[:, 0], u_all.at[x, y, :, :, 512:640]),
-        local(up_kv.at[:, 1], u_all.at[x, y, :, :, 640:768]),
+        local(up_q.at[:, :, 0:256], u_a.at[y, :, :, 0:256]),
+        local(up_kv.at[:, 0], u_a.at[y, :, :, 256:384]),
+        local(up_q.at[:, :, 256:512], u_b.at[x, :, :, 0:256]),
+        local(up_kv.at[:, 1], u_b.at[x, :, :, 256:384]),
     ]
     own_p = local(down_o, p_all.at[x, y])
     own_o = [
@@ -168,6 +174,8 @@
     z_parts = (lambda i: z_all.at[i * 2 + c, 0:64], lambda i: z_all.at[i * 2 + c, 64:128], z, at_z)
     da_parts = (lambda i: d_a.at[i, 0:4], lambda i: d_a.at[i, 4:8], y, at_y)
     db_parts = (lambda i: d_b.at[i, 0:4], lambda i: d_b.at[i, 4:8], x, at_x)
+    ua_parts = (lambda i: u_a.at[i, 0:4], lambda i: u_a.at[i, 4:8], y, at_y)
+    ub_parts = (lambda i: u_b.at[i, 0:4], lambda i: u_b.at[i, 4:8], x, at_x)
     oa_parts = (lambda i: o_a.at[i, 0:4], lambda i: o_a.at[i, 4:8], y, at_y)
     ob_parts = (lambda i: o_b.at[i, 0:4], lambda i: o_b.at[i, 4:8], x, at_x)
 
@@ -195,10 +203,6 @@
             columns = pl.ds(pl.multiple_of(i * 1024, 1024), 1024)
             o_copies.append(local(out_w.at[:, columns], w_out.at[i]))
 
-    for copy in own_u:
-        copy.wait()
-    ua1, ub1 = gather_one(u_all)
-
     ha2 = ring_two(ha1, *ha_parts)
     hb2 = ring_two(hb1, *hb_parts)
     z2 = ring_two(z1, *z_parts)
@@ -206,6 +210,8 @@
     up_z, down_z = wrap(z + 1), wrap(z - 1)
     s1 = send(z_all.at[up_z * 2 + c], z_all.at[up_z * 2 + c], sibling)
     s2 = send(z_all.at[down_z * 2 + c], z_all.at[down_z * 2 + c], sibling)
+    da2 = ring_two(da1, *da_parts)
+    db2 = ring_two(db1, *db_parts)
 
     for copy in w_copies:
         copy.wait()
@@ -233,9 +239,6 @@
     sines = jnp.where(lane < 64, -jnp.sin(angles), jnp.sin(angles))
     owner_ids = column(own_ids[0:1])
 
-    da2 = ring_two(da1, *da_parts)
-    db2 = ring_two(db1, *db_parts)
-    ua2, ub2 = gather_two(u_all, ua1, ub1)
 
     landed(z2)
     far = wrap(z + 2) * 2 + c
@@ -303,71 +306,150 @@
         send(low_send_b.at[wrap(y + d)], low_recv_b.at[y], at_y(d)) for d in (1, 3, 2)
     ]
 
-    landed(ua2 + ub2)
-    ua3, ub3 = gather_three(u_all)
-
+    for copy in own_u:
+        copy.wait()
+    ua1 = ring_one(*ua_parts)
+    ub1 = ring_one(*ub_parts)
+    own_p.wait()
+    pa1, pb1 = gather_one(p_all)
     landed(back_a)
     landed(back_b)
     part = low_send_a[x] + low_send_b[y]
     for d in (1, 2, 3):
         part = part + low_recv_a[wrap(x + d)] + low_recv_b[wrap(y + d)]
-    low_parts[t] = part
-    over_t = [
-        send(low_parts.at[t], low_parts.at[t], (replica, lax.rem(t + d, 8)))
-        for d in range(1, 8)
-    ]
-    own_p.wait()
-    pa1, pb1 = gather_one(p_all)
-    landed(over_t)
+    def over_tensor(part, mine, theirs, parts, forward):
+        mine[...] = part
+        landed([send(mine, theirs, sibling)])
+        parts[z] = part + theirs[...]
+        copies = [send(parts.at[z], parts.at[z], at_z(d)) for d in (2, 1, 3)]
+        forward()
+        landed(copies)
+        return (parts[0] + parts[1]) + (parts[2] + parts[3])
+
+    pools = []
+
+    def forward_pools():
+        pools.append(ring_two(ua1, *ua_parts))
+        pools.append(ring_two(ub1, *ub_parts))
+        pools.extend(gather_two(p_all, pa1, pb1))
+
+    low = over_tensor(part, low_mine, low_theirs, low_parts, forward_pools)
+    ua2, ub2, pa2, pb2 = pools
 
     def spread(low, first):
         source = lax.broadcasted_iota(jnp.int32, (128, 128), 0)
         target = lax.broadcasted_iota(jnp.int32, (128, 128), 1)
-        pattern = (source == first + lax.rem(target, 16)).astype(BF16)
+        pattern = (source == first + lax.rem(target, 16)).astype(F32).astype(BF16)
         return mm(low, pattern)
 
     lane_adapter = (lane // 16).astype(F32)
 
-    def expand(tiled):
-        return jnp.concatenate(
+    def turned(low):
+        padding = jnp.zeros((128 - low.shape[0], 128), F32)
+        full = jnp.concatenate([low.astype(F32), padding], axis=0)
+        return jnp.transpose(full, (1, 0)).astype(BF16)
+
+    class RingSum:
+        def __init__(self, far, half, near, back, device):
+            self.far_block, self.half, self.near_block, self.back = far, half, near, back
+            self.device = device
+
+        def far(self, block):
+            self.far_block[...] = block.astype(BF16)
+            self.halves = [
+                send(self.far_block.at[0:64], self.half.at[0], self.device(1)),
+                send(self.far_block.at[64:128], self.half.at[1], self.device(-1)),
+            ]
+
+        def near(self, plus, minus):
+            near, back = self.near_block, self.back
+            self.waiting = plus[0:64], minus[64:128]
+            near[0, 64:128] = plus[64:128].astype(BF16)
+            near[1, 0:64] = minus[0:64].astype(BF16)
+            self.blocks = [
+                send(near.at[0, 64:128], back.at[0, 64:128], self.device(1)),
+                send(near.at[1, 0:64], back.at[1, 0:64], self.device(-1)),
+            ]
+
+        def join(self):
+            near, back = self.near_block, self.back
+            landed(self.halves[0:1])
+            near[0, 0:64] = (self.waiting[0] + self.half[0].astype(F32)).astype(BF16)
+            self.blocks.append(send(near.at[0, 0:64], back.at[0, 0:64], self.device(1)))
+            landed(self.halves[1:2])
+            near[1, 64:128] = (self.waiting[1] + self.half[1].astype(F32)).astype(BF16)
+            self.blocks.append(send(near.at[1, 64:128], back.at[1, 64:128], self.device(-1)))
+
+        def total(self):
+            landed(self.blocks)
+            return self.back[0].astype(F32) + self.back[1].astype(F32)
+
+    def expand(g, columns, rows, owner):
+        blocks = []
+        for j in range(4):
+            first = (owner(j) * 8).astype(F32)
+            blocks.append(jnp.where(columns[g] == lane_adapter + first, rows, 0.0).astype(BF16))
+        return jnp.concatenate(blocks, axis=1)
+
+    def owner_a(j):
+        return x * 4 + j
+
+    def owner_b(j):
+        return j * 4 + y
+
+    low_a[x] = low.astype(BF16)
+    low_b[y] = low.astype(BF16)
+    around_a = [send(low_a.at[x], low_a.at[x], at_x(d)) for d in (2, 1, 3)]
+    around_b = [send(low_b.at[y], low_b.at[y], at_y(d)) for d in (2, 1, 3)]
+    landed(ua2)
+    landed(ub2)
+
+    def raised(g, columns, lows, first, owner, maps):
+        rows = turned(lows[g])
+        for_q = expand(g, columns, spread(rows, 0), owner)
+        for_kv = expand(g, columns, spread(rows, first), owner)
+        return ADAPTER_SCALE * jnp.concatenate(
             [
-                jnp.where(owner_ids == lane_adapter + 8.0 * i, tiled, 0.0).astype(BF16)
-                for i in range(16)
+                mm(for_q, maps[:, :, :, 0:256].reshape(512, 256)),
+                mm(for_kv, maps[:, :, :, 256:384].reshape(512, 128)),
             ],
             axis=1,
         )
 
-    low = low_parts[0]
-    for i in range(1, 8):
-        low = low + low_parts[i]
-    low = jnp.concatenate([low, jnp.zeros((80, 128), F32)], axis=0)
-    low = jnp.transpose(low, (1, 0)).astype(BF16)
-
-    ua4, ub4 = gather_four(u_all, ua3, ub3)
-    expand_q = expand(spread(low, 0))
-    expand_k = expand(spread(low, 16))
-    expand_v = expand(spread(low, 32))
-
-    pa2, pb2 = gather_two(p_all, pa1, pb1)
-    landed(ua4 + ub4)
+    def raised_a(d):
+        return raised(wrap(x + d), id_columns_a, low_a, 16, owner_a, u_a)
+
+    def raised_b(d):
+        return raised(wrap(y + d), id_columns_b, low_b, 32, owner_b, u_b)
+
+    xu = RingSum(xu_far, xu_half, xu_near, xu_back, at_x)
+    yu = RingSum(yu_far, yu_half, yu_near, yu_back, at_y)
+    landed(around_a[0:1])
+    xu.far(raised_a(2))
+    landed(around_b[0:1])
+    yu.far(raised_b(2))
+    landed(around_a)
+    xu.near(raised_a(1), raised_a(3))
+    landed(around_b)
+    yu.near(raised_b(1), raised_b(3))
+    own_a, own_b = raised_a(0), raised_b(0)
+    xu.join()
+    yu.join()
     landed(pa2 + pb2)
     pa3, pb3 = gather_three(p_all)
     for copy in own_o:
         copy.wait()
-    oa1 = ring_one(*oa_parts)
-    ob1 = ring_one(*ob_parts)
-
-    def raised(expanded, maps, lo, hi):
-        return mm(expanded, maps[:, :, :, :, lo:hi].reshape(2048, hi - lo))
-
-    acc[:, 0:512] += ADAPTER_SCALE * raised(expand_q, u_all, 0, 512)
-    acc[:, 512:640] += ADAPTER_SCALE * raised(expand_k, u_all, 512, 640)
-    acc[:, 640:768] += ADAPTER_SCALE * raised(expand_v, u_all, 640, 768)
+    own_a = own_a + xu.total()
+    acc[:, 0:256] += own_a[:, 0:256]
+    acc[:, 512:640] += own_a[:, 256:384]
+    own_b = own_b + yu.total()
+    acc[:, 256:512] += own_b[:, 0:256]
+    acc[:, 640:768] += own_b[:, 256:384]
 
     def rotated(columns):
         flat = acc[:, columns * 128 : (columns + 1) * 128]
-        turned = flat * cosines + pltpu.roll(flat, 64, 1) * sines
-        return turned.astype(BF16).astype(F32)
+        moved = flat * cosines + pltpu.roll(flat, 64, 1) * sines
+        return moved.astype(BF16).astype(F32)
 
     new_key = rotated(4)
     new_value = acc[:, 640:768].astype(BF16).astype(F32)
@@ -412,11 +494,13 @@
         mixed_rows[rows, :] = jnp.concatenate(mixed, axis=0) + self16 * value_rows[rows, :]
         return 0
 
-    lax.fori_loop(0, 4, attend, 0)
+    lax.fori_loop(0, 3, attend, 0)
     pa4, pb4 = gather_four(p_all, pa3, pb3)
+    oa1 = ring_one(*oa_parts)
+    ob1 = ring_one(*ob_parts)
+    lax.fori_loop(3, 8, attend, 0)
     oa2 = ring_two(oa1, *oa_parts)
     ob2 = ring_two(ob1, *ob_parts)
-    lax.fori_loop(4, 8, attend, 0)
     attended = jnp.concatenate(
         [mixed_rows[pl.ds(i, 128, stride=8), :].astype(BF16) for i in range(4)], axis=1
     )
@@ -430,11 +514,8 @@
         every = every.reshape(32, 16, 128)
         for i in range(32):
             low_out = low_out + jnp.where(own_row == float(j * 32 + i), every[i], 0.0)
-    out_parts[t] = low_out
-    out_over_t = [
-        send(out_parts.at[t], out_parts.at[t], (replica, lax.rem(t + d, 8)))
-        for d in range(1, 8)
-    ]
+    out_mine[...] = low_out
+    to_core = send(out_mine, out_theirs, sibling)
 
     for copy in o_copies:
         copy.wait()
@@ -444,80 +525,57 @@
         sib_send[i] = mm(attended, w_out[i * 2 + other]).astype(BF16)
         to_sibling[d] = send(sib_send.at[i], sib_recv.at[i], sibling)
 
-    landed(out_over_t)
-    low_out = out_parts[0]
-    for i in range(1, 8):
-        low_out = low_out + out_parts[i]
-    low_out = jnp.concatenate([low_out, jnp.zeros((112, 128), F32)], axis=0)
-    low_out = jnp.transpose(low_out, (1, 0)).astype(BF16)
-    tiled = spread(low_out, 0).astype(BF16)
-    low_a[x] = tiled
-    low_b[y] = tiled
-    around_a = [send(low_a.at[x], low_a.at[x], at_x(d)) for d in (2, 1, 3)]
-    around_b = [send(low_b.at[y], low_b.at[y], at_y(d)) for d in (2, 1, 3)]
-
-    def sum_far(block, far, half, device):
-        far[...] = block.astype(BF16)
-        return [
-            send(far.at[0:64], half.at[0], device(1)),
-            send(far.at[64:128], half.at[1], device(-1)),
-        ]
-
-    def sum_near(block, d, halves, half, near, back, device):
-        if d == 1:
-            landed(halves[0:1])
-            near[0, 0:64] = (block[0:64] + half[0].astype(F32)).astype(BF16)
-            near[0, 64:128] = block[64:128].astype(BF16)
-            return send(near.at[0], back.at[0], device(1))
-        landed(halves[1:2])
-        near[1, 0:64] = block[0:64].astype(BF16)
-        near[1, 64:128] = (block[64:128] + half[1].astype(F32)).astype(BF16)
-        return send(near.at[1], back.at[1], device(-1))
-
     def chip_sum(d):
         i = wrap(z + d)
         mine = mm(attended, w_out[i * 2 + c])
         landed([to_sibling[d]])
         return mine + sib_recv[i].astype(F32)
 
-    halves = sum_far(chip_sum(2), z_far, z_half, at_z)
-    z_plus = sum_near(chip_sum(1), 1, halves, z_half, z_near, z_back, at_z)
-    z_minus = sum_near(chip_sum(3), 3, halves, z_half, z_near, z_back, at_z)
+    landed([to_core])
+    out_parts[z] = out_mine[...] + out_theirs[...]
+    out_over_z = [send(out_parts.at[z], out_parts.at[z], at_z(d)) for d in (2, 1, 3)]
+    over_z = RingSum(z_far, z_half, z_near, z_back, at_z)
+    over_z.far(chip_sum(2))
+    over_z.near(chip_sum(1), chip_sum(3))
+
+    landed(out_over_z)
+    low_out = (out_parts[0] + out_parts[1]) + (out_parts[2] + out_parts[3])
+    out_low_a[x] = low_out.astype(BF16)
+    out_low_b[y] = low_out.astype(BF16)
+    around_a = [send(out_low_a.at[x], out_low_a.at[x], at_x(d)) for d in (2, 1, 3)]
+    around_b = [send(out_low_b.at[y], out_low_b.at[y], at_y(d)) for d in (2, 1, 3)]
+    over_z.join()
+
+    def product(g, columns, lows, owner, maps):
+        expanded = expand(g, columns, spread(turned(lows[g]), 0), owner)
+        return ADAPTER_SCALE * mm(expanded, maps[...].reshape(512, 512))
+
+    def product_a(d):
+        return product(wrap(x + d), id_columns_a, out_low_a, owner_a, o_a)
+
+    def product_b(d):
+        return product(wrap(y + d), id_columns_b, out_low_b, owner_b, o_b)
 
     landed(oa2)
     landed(ob2)
+    over_x = RingSum(x_far, x_half, x_near, x_back, at_x)
+    over_y = RingSum(y_far, y_half, y_near, y_back, at_y)
+    landed(around_a[0:1])
+    over_x.far(product_a(2))
+    landed(around_b[0:1])
+    over_y.far(product_b(2))
     landed(around_a)
+    over_x.near(product_a(1), product_a(3))
     landed(around_b)
-
-    def product(g, columns, lows, owner, maps):
-        rows = lows[g].astype(F32)
-        blocks = []
-        for j in range(4):
-            first = (owner(j) * 8).astype(F32)
-            blocks.append(jnp.where(columns[g] == lane_adapter + first, rows, 0.0).astype(BF16))
-        return ADAPTER_SCALE * mm(jnp.concatenate(blocks, axis=1), maps[...].reshape(512, 512))
-
-    def product_a(d):
-        return product(wrap(x + d), id_columns_a, low_a, lambda j: x * 4 + j, o_a)
-
-    def product_b(d):
-        return product(wrap(y + d), id_columns_b, low_b, lambda j: j * 4 + y, o_b)
-
-    halves_a = sum_far(product_a(2), x_far, x_half, at_x)
-    halves_b = sum_far(product_b(2), y_far, y_half, at_y)
-    near_plus_a, near_plus_b = product_a(1), product_b(1)
-    x_plus = sum_near(near_plus_a, 1, halves_a, x_half, x_near, x_back, at_x)
-    y_plus = sum_near(near_plus_b, 1, halves_b, y_half, y_near, y_back, at_y)
-    x_minus = sum_near(product_a(3), 3, halves_a, x_half, x_near, x_back, at_x)
-    y_minus = sum_near(product_b(3), 3, halves_b, y_half, y_near, y_back, at_y)
+    over_y.near(product_b(1), product_b(3))
+    over_x.join()
+    over_y.join()
     own_sum[...] = chip_sum(0)
     own_sum[:, 0:512] += product_a(0)
     own_sum[:, 512:1024] += product_b(0)
-    landed([z_plus, z_minus])
-    own_sum[...] += z_back[0].astype(F32) + z_back[1].astype(F32)
-    landed([x_plus, x_minus, y_plus, y_minus])
-    out[:, 0:512] = own_sum[:, 0:512] + (x_back[0].astype(F32) + x_back[1].astype(F32))
-    out[:, 512:1024] = own_sum[:, 512:1024] + (y_back[0].astype(F32) + y_back[1].astype(F32))
+    own_sum[...] += over_z.total()
+    out[:, 0:512] = own_sum[:, 0:512] + over_x.total()
+    out[:, 512:1024] = own_sum[:, 512:1024] + over_y.total()
 
     for copy in sent:
         copy.wait_send()
@@ -556,7 +614,8 @@
             pltpu.VMEM((4, 144, 512), BF16),
             pltpu.VMEM((4, 8, 48, 512), BF16),
             pltpu.VMEM((4, 8, 48, 512), BF16),
-            pltpu.VMEM((4, 4, 8, 16, 768), BF16),
+            pltpu.VMEM((4, 8, 16, 384), BF16),
+            pltpu.VMEM((4, 8, 16, 384), BF16),
             pltpu.VMEM((4, 4, 8, 16, 512), BF16),
             pltpu.VMEM((4, 8, 16, 512), BF16),
             pltpu.VMEM((4, 8, 16, 512), BF16),
@@ -569,8 +628,12 @@
             pltpu.VMEM((4, 48, 128), F32),
             pltpu.VMEM((4, 48, 128), F32),
             pltpu.VMEM((4, 48, 128), F32),
-            pltpu.VMEM((8, 48, 128), F32),
-            pltpu.VMEM((8, 16, 128), F32),
+            pltpu.VMEM((4, 48, 128), F32),
+            pltpu.VMEM((4, 16, 128), F32),
+            pltpu.VMEM((48, 128), F32),
+            pltpu.VMEM((48, 128), F32),
+            pltpu.VMEM((16, 128), F32),
+            pltpu.VMEM((16, 128), F32),
             pltpu.VMEM((1024, 128), F32),
             pltpu.VMEM((1024, 128), F32),
             pltpu.VMEM((1024, 128), F32),
@@ -585,8 +648,10 @@
             pltpu.VMEM((1, 128), F32),
             pltpu.VMEM((4, 128, 128), F32),
             pltpu.VMEM((4, 128, 128), F32),
-            pltpu.VMEM((4, 128, 128), BF16),
-            pltpu.VMEM((4, 128, 128), BF16),
+            pltpu.VMEM((4, 48, 128), BF16),
+            pltpu.VMEM((4, 48, 128), BF16),
+            pltpu.VMEM((4, 16, 128), BF16),
+            pltpu.VMEM((4, 16, 128), BF16),
             pltpu.VMEM((128, 1024), BF16),
             pltpu.VMEM((2, 64, 1024), BF16),
             pltpu.VMEM((2, 128, 1024), BF16),
@@ -599,6 +664,14 @@
             pltpu.VMEM((2, 64, 512), BF16),
             pltpu.VMEM((2, 128, 512), BF16),
             pltpu.VMEM((2, 128, 512), BF16),
+            pltpu.VMEM((128, 384), BF16),
+            pltpu.VMEM((2, 64, 384), BF16),
+            pltpu.VMEM((2, 128, 384), BF16),
+            pltpu.VMEM((2, 128, 384), BF16),
+            pltpu.VMEM((128, 384), BF16),
+            pltpu.VMEM((2, 64, 384), BF16),
+            pltpu.VMEM((2, 128, 384), BF16),
+            pltpu.VMEM((2, 128, 384), BF16),
             pltpu.SemaphoreType.DMA((SENDS,)),
             pltpu.SemaphoreType.DMA((SENDS,)),
             pltpu.SemaphoreType.DMA((LOCALS,)),

time: 86.4 us -> 80.3 us (0.929)
  Pallas kernels: 84.4 us -> 78.4 us
    pallas_call x1, Pallas kernels: 84.4 us -> 78.4 us  [shards(): pl.pallas_call(kernel, out_shape=jax.ShapeDtypeStruct((128, 1024), F32),...]
where the time goes in v3:
time: 80.3 us; the launch traced here: 80.1 us
  Pallas kernels  78.4 us (98%)
  other arithmetic  1.78 us (2%)
    pallas_call x1, Pallas kernels, shards(): pl.pallas_call(kernel, out_shape=jax.ShapeDtypeStruct((128, 1024), F32),...  78.4 us
    convert_element_type x1, other arithmetic, shards(): return result.astype(BF16)  1.78 us

profile of v3, /device:TPU:0, one launch (start us, length us, event | category | flops | bytes accessed | tf_op | source)
XLA Modules:
  0.0 80.1 jit_solution(3057942340141508505)
XLA Ops:
  0.0 78.4 %shard_map.145 = f32[128,1024]{1,0:T(8,128)} custom-call(bf16[128,1024]{1,0:T(8,128)(2,1)} %hidden.1, s32[16,32]{1,0:T(8,128)} %lists.1, s32[1,128]{1,0:T(1,128)} %bitcast.14, s32[1,128]{1,0:T(1,128)} %bitcast.15, f32[1,128]{1,0:T(1,128)} %constant.2.clone.frequencies, bf16[8,1024,512]{2,1,0:T(8,128)(2,1)} %bitcast.8, bf16[2,8,1024,128]{3,2,1,0:T(8,128)(2,1)} %bitcast.9, ...), custom_call_target="tpu_custom_call" | custom-call | flops 8000000000 | bytes 32000000 | tf_op jit(solution)/shard_map/pallas_call | solution.py:606
  78.4 1.8 %convert_element_type.3 = bf16[128,1024]{1,0:T(8,128)(2,1)} convert(f32[128,1024]{1,0:T(8,128)} %shard_map.145) | non-fusion elementwise | flops 131072 | bytes 786432 | tf_op jit(solution)/shard_map/convert_element_type | solution.py:700

commit v4 on v3

--- a/solution.py
+++ b/solution.py
@@ -129,13 +129,17 @@
                 arrived.add(id(copy))
                 copy.wait_recv()
 
+    def ring_rest(lo, hi, own, device):
+        return [
+            send(hi(own), hi(own), device(1)),
+            send(lo(own), lo(own), device(-1)),
+        ]
+
     def ring_one(lo, hi, own, device):
         return [
             send(lo(own), lo(own), device(1)),
             send(hi(own), hi(own), device(-1)),
-            send(hi(own), hi(own), device(1)),
-            send(lo(own), lo(own), device(-1)),
-        ]
+        ] + ring_rest(lo, hi, own, device)
 
     def ring_two(first, lo, hi, own, device):
         before, after = wrap(own - 1), wrap(own + 1)
@@ -160,10 +164,6 @@
     def gather_two(pool, a, b):
         parts = pool_parts(pool)
         return ring_two(a, *parts[0]), ring_two(b, *parts[1])
-
-    def gather_three(pool):
-        parts = pool_parts(pool)
-        return ring_one(*parts[2]), ring_one(*parts[3])
 
     def gather_four(pool, a, b):
         parts = pool_parts(pool)
@@ -401,6 +401,21 @@
     low_b[y] = low.astype(BF16)
     around_a = [send(low_a.at[x], low_a.at[x], at_x(d)) for d in (2, 1, 3)]
     around_b = [send(low_b.at[y], low_b.at[y], at_y(d)) for d in (2, 1, 3)]
+    landed(pa2 + pb2)
+
+    def early(lo, hi):
+        return (
+            [
+                send(p_all.at[lo:hi, y, 0:2], p_all.at[lo:hi, y, 0:2], at_y(1)),
+                send(p_all.at[lo:hi, y, 2:4], p_all.at[lo:hi, y, 2:4], at_y(-1)),
+            ],
+            [
+                send(p_all.at[x, lo:hi, 4:6], p_all.at[x, lo:hi, 4:6], at_x(1)),
+                send(p_all.at[x, lo:hi, 6:8], p_all.at[x, lo:hi, 6:8], at_x(-1)),
+            ],
+        )
+
+    pa3, pb3 = early(0, 2)
     landed(ua2)
     landed(ub2)
 
@@ -428,6 +443,8 @@
     xu.far(raised_a(2))
     landed(around_b[0:1])
     yu.far(raised_b(2))
+    more_a, more_b = early(2, 4)
+    pa3, pb3 = pa3 + more_a, pb3 + more_b
     landed(around_a)
     xu.near(raised_a(1), raised_a(3))
     landed(around_b)
@@ -435,10 +452,13 @@
     own_a, own_b = raised_a(0), raised_b(0)
     xu.join()
     yu.join()
-    landed(pa2 + pb2)
-    pa3, pb3 = gather_three(p_all)
+    landed(pa3 + pb3)
+    pa4, pb4 = gather_four(p_all, pa3, pb3)
+    pa4, pb4 = pa4 + ring_rest(*pool_parts(p_all)[2]), pb4 + ring_rest(*pool_parts(p_all)[3])
     for copy in own_o:
         copy.wait()
+    oa1 = ring_one(*oa_parts)
+    ob1 = ring_one(*ob_parts)
     own_a = own_a + xu.total()
     acc[:, 0:256] += own_a[:, 0:256]
     acc[:, 512:640] += own_a[:, 256:384]
@@ -465,20 +485,20 @@
     scale = 1.0 / (128.0 ** 0.5)
 
     def attend(b, _):
-        first = pl.multiple_of(b * 128, 128)
-        rows = pl.ds(first, 128)
+        first = pl.multiple_of(b * 256, 256)
+        rows = pl.ds(first, 256)
         q = q_rows[rows, :]
         q16 = q.astype(BF16)
         scores = []
-        for i in range(16):
+        for i in range(32):
             scores.append(
                 lax.dot_general(
-                    q16[i * 8 : (i + 1) * 8], k_all[b * 16 + i], NT, preferred_element_type=F32
+                    q16[i * 8 : (i + 1) * 8], k_all[b * 32 + i], NT, preferred_element_type=F32
                 )
             )
         scores = jnp.concatenate(scores, axis=0) * scale
         self_score = jnp.sum(q * key_rows[rows, :], axis=1, keepdims=True) * scale
-        slot = lax.broadcasted_iota(jnp.int32, (128, 128), 1).astype(F32)
+        slot = lax.broadcasted_iota(jnp.int32, (256, 128), 1).astype(F32)
         valid = slot < length_rows[rows, :]
         highest = jnp.maximum(
             jnp.max(jnp.where(valid, scores, NEGATIVE), axis=1, keepdims=True), self_score
@@ -489,16 +509,12 @@
         weights16 = (weights / total).astype(BF16)
         self16 = (self_weight / total).astype(BF16).astype(F32)
         mixed = []
-        for i in range(16):
-            mixed.append(mm(weights16[i * 8 : (i + 1) * 8], v_all[b * 16 + i]))
+        for i in range(32):
+            mixed.append(mm(weights16[i * 8 : (i + 1) * 8], v_all[b * 32 + i]))
         mixed_rows[rows, :] = jnp.concatenate(mixed, axis=0) + self16 * value_rows[rows, :]
         return 0
 
-    lax.fori_loop(0, 3, attend, 0)
-    pa4, pb4 = gather_four(p_all, pa3, pb3)
-    oa1 = ring_one(*oa_parts)
-    ob1 = ring_one(*ob_parts)
-    lax.fori_loop(3, 8, attend, 0)
+    lax.fori_loop(0, 4, attend, 0)
     oa2 = ring_two(oa1, *oa_parts)
     ob2 = ring_two(ob1, *ob_parts)
     attended = jnp.concatenate(

time: 80.3 us -> 77.9 us (0.970)
  Pallas kernels: 78.4 us -> 75.9 us
    pallas_call x1, Pallas kernels: 78.4 us -> 75.9 us  [shards(): pl.pallas_call(kernel, out_shape=jax.ShapeDtypeStruct((128, 1024), F32),...]
where the time goes in v4:
time: 77.9 us; the launch traced here: 77.7 us
  Pallas kernels  75.9 us (97%)
  other arithmetic  1.78 us (2%)
    pallas_call x1, Pallas kernels, shards(): pl.pallas_call(kernel, out_shape=jax.ShapeDtypeStruct((128, 1024), F32),...  75.9 us
    convert_element_type x1, other arithmetic, shards(): return result.astype(BF16)  1.78 us

profile of v4, /device:TPU:0, one launch (start us, length us, event | category | flops | bytes accessed | tf_op | source)
XLA Modules:
  0.0 77.7 jit_solution(4875332112607198931)
XLA Ops:
  0.0 75.9 %shard_map.145 = f32[128,1024]{1,0:T(8,128)} custom-call(bf16[128,1024]{1,0:T(8,128)(2,1)} %hidden.1, s32[16,32]{1,0:T(8,128)} %lists.1, s32[1,128]{1,0:T(1,128)} %bitcast.14, s32[1,128]{1,0:T(1,128)} %bitcast.15, f32[1,128]{1,0:T(1,128)} %constant.2.clone.frequencies, bf16[8,1024,512]{2,1,0:T(8,128)(2,1)} %bitcast.8, bf16[2,8,1024,128]{3,2,1,0:T(8,128)(2,1)} %bitcast.9, ...), custom_call_target="tpu_custom_call" | custom-call | flops 8000000000 | bytes 32000000 | tf_op jit(solution)/shard_map/pallas_call | solution.py:622
  75.9 1.8 %convert_element_type.3 = bf16[128,1024]{1,0:T(8,128)(2,1)} convert(f32[128,1024]{1,0:T(8,128)} %shard_map.145) | non-fusion elementwise | flops 131072 | bytes 786432 | tf_op jit(solution)/shard_map/convert_element_type | solution.py:716

commit v5 on v4

--- a/solution.py
+++ b/solution.py
@@ -237,7 +237,8 @@
     lane = lax.broadcasted_iota(jnp.int32, (128, 128), 1)
     cosines = jnp.cos(angles)
     sines = jnp.where(lane < 64, -jnp.sin(angles), jnp.sin(angles))
-    owner_ids = column(own_ids[0:1])
+    for i in range(8):
+        length_rows[pl.ds(i, 128, stride=8), :] = row_lengths
 
 
     landed(z2)
@@ -306,35 +307,53 @@
         send(low_send_b.at[wrap(y + d)], low_recv_b.at[y], at_y(d)) for d in (1, 3, 2)
     ]
 
+    own_p.wait()
+    pa1, pb1 = gather_one(p_all)
     for copy in own_u:
         copy.wait()
     ua1 = ring_one(*ua_parts)
     ub1 = ring_one(*ub_parts)
-    own_p.wait()
-    pa1, pb1 = gather_one(p_all)
     landed(back_a)
     landed(back_b)
     part = low_send_a[x] + low_send_b[y]
     for d in (1, 2, 3):
         part = part + low_recv_a[wrap(x + d)] + low_recv_b[wrap(y + d)]
-    def over_tensor(part, mine, theirs, parts, forward):
+    def over_tensor(part, mine, theirs, parts, forward_first, forward):
         mine[...] = part
-        landed([send(mine, theirs, sibling)])
+        to_core = send(mine, theirs, sibling)
+        forward_first()
+        landed([to_core])
         parts[z] = part + theirs[...]
         copies = [send(parts.at[z], parts.at[z], at_z(d)) for d in (2, 1, 3)]
         forward()
         landed(copies)
         return (parts[0] + parts[1]) + (parts[2] + parts[3])
 
+    def piece(lo, hi, first, second):
+        return (
+            [
+                send(p_all.at[lo:hi, y, first : first + 2], p_all.at[lo:hi, y, first : first + 2], at_y(1)),
+                send(p_all.at[lo:hi, y, second : second + 2], p_all.at[lo:hi, y, second : second + 2], at_y(-1)),
+            ],
+            [
+                send(p_all.at[x, lo:hi, first + 4 : first + 6], p_all.at[x, lo:hi, first + 4 : first + 6], at_x(1)),
+                send(p_all.at[x, lo:hi, second + 4 : second + 6], p_all.at[x, lo:hi, second + 4 : second + 6], at_x(-1)),
+            ],
+        )
+
     pools = []
 
-    def forward_pools():
+    def forward_p():
+        pools.extend(gather_two(p_all, pa1, pb1))
+
+    def forward_u():
         pools.append(ring_two(ua1, *ua_parts))
         pools.append(ring_two(ub1, *ub_parts))
-        pools.extend(gather_two(p_all, pa1, pb1))
-
-    low = over_tensor(part, low_mine, low_theirs, low_parts, forward_pools)
-    ua2, ub2, pa2, pb2 = pools
+        landed(pools[0] + pools[1])
+        pools.extend(piece(0, 2, 0, 2))
+
+    low = over_tensor(part, low_mine, low_theirs, low_parts, forward_p, forward_u)
+    pa2, pb2, ua2, ub2, pa3, pb3 = pools
 
     def spread(low, first):
         source = lax.broadcasted_iota(jnp.int32, (128, 128), 0)
@@ -401,21 +420,8 @@
     low_b[y] = low.astype(BF16)
     around_a = [send(low_a.at[x], low_a.at[x], at_x(d)) for d in (2, 1, 3)]
     around_b = [send(low_b.at[y], low_b.at[y], at_y(d)) for d in (2, 1, 3)]
-    landed(pa2 + pb2)
-
-    def early(lo, hi):
-        return (
-            [
-                send(p_all.at[lo:hi, y, 0:2], p_all.at[lo:hi, y, 0:2], at_y(1)),
-                send(p_all.at[lo:hi, y, 2:4], p_all.at[lo:hi, y, 2:4], at_y(-1)),
-            ],
-            [
-                send(p_all.at[x, lo:hi, 4:6], p_all.at[x, lo:hi, 4:6], at_x(1)),
-                send(p_all.at[x, lo:hi, 6:8], p_all.at[x, lo:hi, 6:8], at_x(-1)),
-            ],
-        )
-
-    pa3, pb3 = early(0, 2)
+    more_a, more_b = piece(2, 4, 0, 2)
+    pa3, pb3 = pa3 + more_a, pb3 + more_b
     landed(ua2)
     landed(ub2)
 
@@ -443,8 +449,7 @@
     xu.far(raised_a(2))
     landed(around_b[0:1])
     yu.far(raised_b(2))
-    more_a, more_b = early(2, 4)
-    pa3, pb3 = pa3 + more_a, pb3 + more_b
+    rest_a, rest_b = piece(0, 2, 2, 0)
     landed(around_a)
     xu.near(raised_a(1), raised_a(3))
     landed(around_b)
@@ -454,7 +459,8 @@
     yu.join()
     landed(pa3 + pb3)
     pa4, pb4 = gather_four(p_all, pa3, pb3)
-    pa4, pb4 = pa4 + ring_rest(*pool_parts(p_all)[2]), pb4 + ring_rest(*pool_parts(p_all)[3])
+    more_a, more_b = piece(2, 4, 2, 0)
+    pa4, pb4 = pa4 + rest_a + more_a, pb4 + rest_b + more_b
     for copy in own_o:
         copy.wait()
     oa1 = ring_one(*oa_parts)
@@ -478,7 +484,6 @@
         q_rows[rows, :] = rotated(i % 4)
         key_rows[rows, :] = new_key
         value_rows[rows, :] = new_value
-        length_rows[rows, :] = row_lengths
 
     k_copy.wait()
     v_copy.wait()
@@ -490,12 +495,13 @@
         q = q_rows[rows, :]
         q16 = q.astype(BF16)
         scores = []
-        for i in range(32):
-            scores.append(
-                lax.dot_general(
-                    q16[i * 8 : (i + 1) * 8], k_all[b * 32 + i], NT, preferred_element_type=F32
-                )
+        for i in range(16):
+            pair = k_all[pl.ds(b * 32 + 2 * i, 2)].reshape(256, 128)
+            both = lax.dot_general(
+                q16[i * 16 : (i + 1) * 16], pair, NT, preferred_element_type=F32
             )
+            scores.append(both[0:8, 0:128])
+            scores.append(both[8:16, 128:256])
         scores = jnp.concatenate(scores, axis=0) * scale
         self_score = jnp.sum(q * key_rows[rows, :], axis=1, keepdims=True) * scale
         slot = lax.broadcasted_iota(jnp.int32, (256, 128), 1).astype(F32)
@@ -506,20 +512,33 @@
         weights = jnp.where(valid, jnp.exp(scores - highest), 0.0)
         self_weight = jnp.exp(self_score - highest)
         total = jnp.sum(weights, axis=1, keepdims=True) + self_weight
-        weights16 = (weights / total).astype(BF16)
+        weights = weights / total
+        even = lax.rem(lax.broadcasted_iota(jnp.int32, (256, 128), 0), 16) < 8
+        weights16 = jnp.concatenate(
+            [jnp.where(even, weights, 0.0), jnp.where(even, 0.0, weights)], axis=1
+        ).astype(BF16)
         self16 = (self_weight / total).astype(BF16).astype(F32)
         mixed = []
-        for i in range(32):
-            mixed.append(mm(weights16[i * 8 : (i + 1) * 8], v_all[b * 32 + i]))
+        for i in range(16):
+            pair = v_all[pl.ds(b * 32 + 2 * i, 2)].reshape(256, 128)
+            mixed.append(mm(weights16[i * 16 : (i + 1) * 16], pair))
         mixed_rows[rows, :] = jnp.concatenate(mixed, axis=0) + self16 * value_rows[rows, :]
         return 0
 
     lax.fori_loop(0, 4, attend, 0)
-    oa2 = ring_two(oa1, *oa_parts)
-    ob2 = ring_two(ob1, *ob_parts)
     attended = jnp.concatenate(
         [mixed_rows[pl.ds(i, 128, stride=8), :].astype(BF16) for i in range(4)], axis=1
     )
+
+    before_output = len(sent)
+
+    for copy in o_copies:
+        copy.wait()
+    to_sibling = {}
+    for d in (2, 1, 3, 0):
+        i = wrap(z + d)
+        sib_send[i] = mm(attended, w_out[i * 2 + other]).astype(BF16)
+        to_sibling[d] = send(sib_send.at[i], sib_recv.at[i], sibling)
 
     landed(pa4 + pb4)
     own_row = own_ids[0:1]
@@ -533,20 +552,14 @@
     out_mine[...] = low_out
     to_core = send(out_mine, out_theirs, sibling)
 
-    for copy in o_copies:
-        copy.wait()
-    to_sibling = {}
-    for d in (2, 1, 3, 0):
-        i = wrap(z + d)
-        sib_send[i] = mm(attended, w_out[i * 2 + other]).astype(BF16)
-        to_sibling[d] = send(sib_send.at[i], sib_recv.at[i], sibling)
-
     def chip_sum(d):
         i = wrap(z + d)
         mine = mm(attended, w_out[i * 2 + c])
         landed([to_sibling[d]])
         return mine + sib_recv[i].astype(F32)
 
+    oa2 = ring_two(oa1, *oa_parts)
+    ob2 = ring_two(ob1, *ob_parts)
     landed([to_core])
     out_parts[z] = out_mine[...] + out_theirs[...]
     out_over_z = [send(out_parts.at[z], out_parts.at[z], at_z(d)) for d in (2, 1, 3)]
@@ -560,6 +573,8 @@
     out_low_b[y] = low_out.astype(BF16)
     around_a = [send(out_low_a.at[x], out_low_a.at[x], at_x(d)) for d in (2, 1, 3)]
     around_b = [send(out_low_b.at[y], out_low_b.at[y], at_y(d)) for d in (2, 1, 3)]
+    for copy in sent[:before_output]:
+        copy.wait_send()
     over_z.join()
 
     def product(g, columns, lows, owner, maps):
@@ -593,7 +608,7 @@
     out[:, 0:512] = own_sum[:, 0:512] + over_x.total()
     out[:, 512:1024] = own_sum[:, 512:1024] + over_y.total()
 
-    for copy in sent:
+    for copy in sent[before_output:]:
         copy.wait_send()
 
 

time: 77.9 us -> 76.1 us (0.977)
  Pallas kernels: 75.9 us -> 74.2 us
    pallas_call x1, Pallas kernels: 75.9 us -> 74.2 us  [shards(): pl.pallas_call(kernel, out_shape=jax.ShapeDtypeStruct((128, 1024), F32),...]
where the time goes in v5:
time: 76.1 us; the launch traced here: 76 us
  Pallas kernels  74.2 us (98%)
  other arithmetic  1.78 us (2%)
    pallas_call x1, Pallas kernels, shards(): pl.pallas_call(kernel, out_shape=jax.ShapeDtypeStruct((128, 1024), F32),...  74.2 us
    convert_element_type x1, other arithmetic, shards(): return result.astype(BF16)  1.78 us

profile of v5, /device:TPU:0, one launch (start us, length us, event | category | flops | bytes accessed | tf_op | source)
XLA Modules:
  0.0 76.0 jit_solution(10349967361181521266)
XLA Ops:
  0.0 74.2 %shard_map.145 = f32[128,1024]{1,0:T(8,128)} custom-call(bf16[128,1024]{1,0:T(8,128)(2,1)} %hidden.1, s32[16,32]{1,0:T(8,128)} %lists.1, s32[1,128]{1,0:T(1,128)} %bitcast.14, s32[1,128]{1,0:T(1,128)} %bitcast.15, f32[1,128]{1,0:T(1,128)} %constant.2.clone.frequencies, bf16[8,1024,512]{2,1,0:T(8,128)(2,1)} %bitcast.8, bf16[2,8,1024,128]{3,2,1,0:T(8,128)(2,1)} %bitcast.9, ...), custom_call_target="tpu_custom_call" | custom-call | flops 8000000000 | bytes 32000000 | tf_op jit(solution)/shard_map/pallas_call | solution.py:637
  74.2 1.8 %convert_element_type.3 = bf16[128,1024]{1,0:T(8,128)(2,1)} convert(f32[128,1024]{1,0:T(8,128)} %shard_map.145) | non-fusion elementwise | flops 131072 | bytes 786432 | tf_op jit(solution)/shard_map/convert_element_type | solution.py:731

commit v6 on v5

--- a/solution.py
+++ b/solution.py
@@ -15,7 +15,7 @@
 F32 = jnp.float32
 NT = (((1,), (1,)), ((), ()))
 NEGATIVE = -1e30
-SENDS = 160
+SENDS = 176
 LOCALS = 64
 
 
@@ -29,7 +29,7 @@
     out,
     z_all, h_a, h_b, d_a, d_b, u_a, u_b, p_all, o_a, o_b, w_all, w_out, k_all, v_all,
     acc, low_send_a, low_recv_a, low_send_b, low_recv_b, low_parts, out_parts,
-    low_mine, low_theirs, out_mine, out_theirs,
+    low_mine, low_theirs,
     q_rows, key_rows, value_rows, length_rows, mixed_rows,
     sib_send, sib_recv, own_sum, lists_v, slots_v, lengths_v, frequencies_v, id_columns_a, id_columns_b,
     low_a, low_b, out_low_a, out_low_b, *sums,
@@ -82,7 +82,7 @@
 
     barrier = pltpu.get_barrier_semaphore()
     partners = [at_x(d) for d in (1, 2, 3)] + [at_y(d) for d in (1, 2, 3)]
-    partners += [at_z(d) for d in (1, 2, 3)] + [sibling]
+    partners += [(replica, lax.rem(t + i, 8)) for i in range(1, 8)]
     for partner in partners:
         pl.semaphore_signal(barrier, inc=1, device_id=partner, device_id_type=MESH)
 
@@ -549,8 +549,10 @@
         every = every.reshape(32, 16, 128)
         for i in range(32):
             low_out = low_out + jnp.where(own_row == float(j * 32 + i), every[i], 0.0)
-    out_mine[...] = low_out
-    to_core = send(out_mine, out_theirs, sibling)
+    out_parts[t] = low_out
+    out_over_t = [
+        send(out_parts.at[t], out_parts.at[t], (replica, lax.rem(t + i, 8))) for i in range(1, 8)
+    ]
 
     def chip_sum(d):
         i = wrap(z + d)
@@ -560,15 +562,14 @@
 
     oa2 = ring_two(oa1, *oa_parts)
     ob2 = ring_two(ob1, *ob_parts)
-    landed([to_core])
-    out_parts[z] = out_mine[...] + out_theirs[...]
-    out_over_z = [send(out_parts.at[z], out_parts.at[z], at_z(d)) for d in (2, 1, 3)]
     over_z = RingSum(z_far, z_half, z_near, z_back, at_z)
     over_z.far(chip_sum(2))
     over_z.near(chip_sum(1), chip_sum(3))
 
-    landed(out_over_z)
-    low_out = (out_parts[0] + out_parts[1]) + (out_parts[2] + out_parts[3])
+    landed(out_over_t)
+    low_out = out_parts[0]
+    for i in range(1, 8):
+        low_out = low_out + out_parts[i]
     out_low_a[x] = low_out.astype(BF16)
     out_low_b[y] = low_out.astype(BF16)
     around_a = [send(out_low_a.at[x], out_low_a.at[x], at_x(d)) for d in (2, 1, 3)]
@@ -660,11 +661,9 @@
             pltpu.VMEM((4, 48, 128), F32),
             pltpu.VMEM((4, 48, 128), F32),
             pltpu.VMEM((4, 48, 128), F32),
-            pltpu.VMEM((4, 16, 128), F32),
+            pltpu.VMEM((8, 16, 128), F32),
             pltpu.VMEM((48, 128), F32),
             pltpu.VMEM((48, 128), F32),
-            pltpu.VMEM((16, 128), F32),
-            pltpu.VMEM((16, 128), F32),
             pltpu.VMEM((1024, 128), F32),
             pltpu.VMEM((1024, 128), F32),
             pltpu.VMEM((1024, 128), F32),

time: 76.1 us -> 76.3 us (level)
  no operation moved by 1% of the time
where the time goes in v6:
time: 76.3 us; the launch traced here: 76.1 us
  Pallas kernels  74.4 us (98%)
  other arithmetic  1.78 us (2%)
    pallas_call x1, Pallas kernels, shards(): pl.pallas_call(kernel, out_shape=jax.ShapeDtypeStruct((128, 1024), F32),...  74.4 us
    convert_element_type x1, other arithmetic, shards(): return result.astype(BF16)  1.78 us

profile of v6, /device:TPU:0, one launch (start us, length us, event | category | flops | bytes accessed | tf_op | source)
XLA Modules:
  0.0 76.1 jit_solution(7142498990799804996)
XLA Ops:
  0.0 74.4 %shard_map.145 = f32[128,1024]{1,0:T(8,128)} custom-call(bf16[128,1024]{1,0:T(8,128)(2,1)} %hidden.1, s32[16,32]{1,0:T(8,128)} %lists.1, s32[1,128]{1,0:T(1,128)} %bitcast.14, s32[1,128]{1,0:T(1,128)} %bitcast.15, f32[1,128]{1,0:T(1,128)} %constant.2.clone.frequencies, bf16[8,1024,512]{2,1,0:T(8,128)(2,1)} %bitcast.8, bf16[2,8,1024,128]{3,2,1,0:T(8,128)(2,1)} %bitcast.9, ...), custom_call_target="tpu_custom_call" | custom-call | flops 8000000000 | bytes 32000000 | tf_op jit(solution)/shard_map/pallas_call | solution.py:638
  74.4 1.8 %convert_element_type.3 = bf16[128,1024]{1,0:T(8,128)(2,1)} convert(f32[128,1024]{1,0:T(8,128)} %shard_map.145) | non-fusion elementwise | flops 131072 | bytes 786432 | tf_op jit(solution)/shard_map/convert_element_type | solution.py:730
